TPU v7x, 32 devices: a whole 2x2x4 slice. The times are simulated.
32 devices in a mesh: ctx: 8 (over y, x, core), ch: 4 (over z).
Axes of the slice: x: 2, y: 2, z: 4, core: 2. Of those that a mesh axis runs over, the one named last changes fastest.
Arguments:
- hidden: bfloat16 [8192, 8192], P('ch', 'ctx'), may hold values from -24 to 24
- cotangent: bfloat16 [8192, 8192], P('ch', 'ctx'), may hold values from -24 to 24
- norm_gain: float32 [8192], P('ch'), may hold values from 0.5 to 1.5
- mr_filter: bfloat16 [512, 128], P('ch'), may hold values from -0.5 to 0.5
- residue: float32 [512, 16], P('ch'), may hold values from -1.5 to 1.5
- decay_rate: float32 [512, 16], P('ch'), may hold values from 1.9073486e-06 to 0.033
- skip_weight: float32 [8192], P('ch'), may hold values from -3 to 3
Outputs:
- grad_hidden: bfloat16 [8192, 8192], P('ch', 'ctx')
- grad_gain: float32 [8192], P('ch')
- grad_mr: float32 [512, 128], P('ch')
- grad_residue: float32 [512, 16], P('ch')
- grad_log_rate: float32 [512, 16], P('ch')
- grad_skip: float32 [8192], P('ch')
- grad_inv_rms: float32 [8192], P('ctx')
All inputs are finite; a program needn't handle non-finite values.
Results may differ from a plain program's by a relative error of at most 0.005.
Values may be sent and summed in bfloat16 or wider, within the bound.
A program may use at most 192 MiB of HBM per device.

v0:
```python
import jax
import jax.numpy as jnp
from jax import lax
from jax.sharding import PartitionSpec as P

eps_norm = 1e-06
top_precision = lax.Precision.HIGHEST


def passed_along(x, axis, by):
    count = lax.axis_size(axis)
    pairs = [(i, i + by) for i in range(count) if 0 <= i + by < count]
    return lax.ppermute(x, axis, pairs)


def tap_table(weights, tap_count):
    row_index = jnp.arange(tap_count)[:, None]
    col_index = jnp.arange(2 * tap_count)[None, :]
    lag_index = tap_count + row_index - col_index
    onehot = (lag_index[None, :, :] == jnp.arange(tap_count)[:, None, None]).astype(jnp.bfloat16)
    tap_matrix = jnp.einsum(
        "gk,kij->gij", weights, onehot, preferred_element_type=jnp.float32
    ).astype(jnp.bfloat16)
    return (tap_matrix, onehot)


def pair_blocks(joined, groups, tap_count):
    channels = joined.shape[0]
    blocks = joined.reshape(groups, channels // groups, joined.shape[1] // tap_count, tap_count)
    return jnp.concatenate([blocks[:, :, :-1], blocks[:, :, 1:]], axis=3)


def block_states(rates, grads_wide, steps):
    falling = jnp.exp(-rates[:, :, None] * steps[None, None, :])
    state_zero = jnp.einsum("gnj,gcbj->gbnc", falling, grads_wide, precision=top_precision)
    state_one = jnp.einsum("gnj,gcbj->gbnc", falling * steps, grads_wide, precision=top_precision)
    return (state_zero, state_one)


def span_suffix(rates, state_zero, state_one, incoming, block_len):
    block_count = state_zero.shape[1]
    positions = jnp.arange(block_count)
    distance = positions[None, :] - positions[:, None] - 1
    lag_blocks = (jnp.maximum(distance, 0) * block_len).astype(jnp.float32)
    coefficient = jnp.where(
        distance[None, None] >= 0, jnp.exp(-rates[:, :, None, None] * lag_blocks[None, None]), 0.0
    )
    later_zero = jnp.einsum("gnbk,gknc->gbnc", coefficient, state_zero, precision=top_precision)
    later_one = jnp.einsum("gnbk,gknc->gbnc", coefficient, state_one, precision=top_precision)
    later_one = later_one + jnp.einsum(
        "gnbk,gknc->gbnc", coefficient * lag_blocks[None, None], state_zero, precision=top_precision
    )
    remaining = ((block_count - 1 - positions) * block_len).astype(jnp.float32)
    lifting = jnp.exp(-rates[:, None, :] * remaining[None, :, None])[..., None]
    after_zero = later_zero + lifting * incoming[:, None]
    after_one = later_one + lifting * (remaining[None, :, None, None] * incoming[:, None])
    return (after_zero, after_one)


def long_tile(mixed_blocks, grad_blocks, rates, residues, after_zero, after_one):
    block_len = mixed_blocks.shape[3]
    steps = jnp.arange(block_len, dtype=jnp.float32)
    falling = jnp.exp(-rates[:, :, None] * steps)
    rising = jnp.exp(rates[:, :, None] * steps)
    to_end = jnp.exp(-rates[:, :, None] * (block_len - steps))
    amplitude = residues * jnp.sqrt(2.0 * rates)
    lower = steps[:, None] >= steps[None, :]
    kernel = jnp.einsum(
        "gni,gnj->gij", amplitude[:, :, None] * falling, rising, precision=top_precision
    )
    kernel = jnp.where(lower[None], kernel, 0.0)
    grads_wide = grad_blocks.astype(jnp.float32)
    inner = jnp.einsum("gij,gcbi->gcbj", kernel, grads_wide, precision=top_precision)
    outer = jnp.einsum(
        "gnj,gbnc->gcbj", amplitude[:, :, None] * to_end, after_zero, precision=top_precision
    )
    pair_sums = jnp.einsum(
        "gcbi,gcbj->gij", grad_blocks, mixed_blocks, preferred_element_type=jnp.float32
    )
    pair_sums = jnp.where(lower[None], pair_sums, 0.0)
    lag_gap = steps[:, None] - steps[None, :]
    near_zero = jnp.einsum("gni,gij,gnj->gn", falling, pair_sums, rising, precision=top_precision)
    near_one = jnp.einsum(
        "gni,gij,gnj->gn", falling, pair_sums * lag_gap[None], rising, precision=top_precision
    )
    mixed_wide = mixed_blocks.astype(jnp.float32)
    lifted = jnp.einsum("gnj,gcbj->gbnc", to_end, mixed_wide, precision=top_precision)
    lifted_one = jnp.einsum(
        "gnj,gcbj->gbnc", to_end * (block_len - steps), mixed_wide, precision=top_precision
    )
    far_zero = jnp.sum(lifted * after_zero, axis=(1, 3))
    far_one = jnp.sum(lifted_one * after_zero + lifted * after_one, axis=(1, 3))
    return (inner + outer, near_zero + far_zero, near_one + far_one)


def local(hidden, cotangent, norm_gain, mr_filter, residue, decay_rate, skip_weight):
    channels, tokens = hidden.shape
    groups = mr_filter.shape[0]
    group_width = channels // groups
    tap_count = mr_filter.shape[1]
    mode_count = residue.shape[1]
    full_width = channels * lax.axis_size("ch")
    seq_length = tokens * lax.axis_size("ctx")
    grad_scale = seq_length ** (-0.5)
    block_len = min(512, tokens)
    hidden_wide = hidden.astype(jnp.float32)
    squares = lax.psum(jnp.sum(hidden_wide * hidden_wide, axis=0), "ch")
    inverse_rms = lax.rsqrt(squares / full_width + eps_norm)
    normed = hidden_wide * inverse_rms[None, :]
    normal_unit = (normed * norm_gain[:, None]).astype(jnp.bfloat16)
    tap_matrix, onehot = tap_table(mr_filter, tap_count)
    edge_rows = passed_along(normal_unit[:, tokens - tap_count :], "ctx", 1)
    window = pair_blocks(jnp.concatenate([edge_rows, normal_unit], axis=1), groups, tap_count)
    mixed = (
        jnp.einsum("gij,gcsj->gcsi", tap_matrix, window, preferred_element_type=jnp.float32)
        .astype(jnp.bfloat16)
        .reshape(channels, tokens)
    )
    mixed_seq, grads_seq = (
        lax.all_to_all(mixed, "ctx", split_axis=0, concat_axis=1, tiled=True),
        lax.all_to_all(cotangent, "ctx", split_axis=0, concat_axis=1, tiled=True),
    )
    local_channels = mixed_seq.shape[0]
    local_groups = local_channels // group_width
    rank_ctx = lax.axis_index("ctx")
    rates_local = lax.dynamic_slice_in_dim(decay_rate, rank_ctx * local_groups, local_groups, 0)
    residues_local = lax.dynamic_slice_in_dim(residue, rank_ctx * local_groups, local_groups, 0)
    skips_local = lax.dynamic_slice_in_dim(
        skip_weight, rank_ctx * local_channels, local_channels, 0
    )
    block_count = mixed_seq.shape[1] // block_len
    mixed_blocks = mixed_seq.reshape(local_groups, group_width, block_count, block_len)
    grad_blocks = grads_seq.reshape(local_groups, group_width, block_count, block_len)
    grads_wide = grads_seq.astype(jnp.float32)
    steps = jnp.arange(block_len, dtype=jnp.float32)
    state_zero, state_one = block_states(
        rates_local, grads_wide.reshape(local_groups, group_width, block_count, block_len), steps
    )
    nothing = jnp.zeros((local_groups, mode_count, group_width), jnp.float32)
    after_zero, after_one = span_suffix(rates_local, state_zero, state_one, nothing, block_len)
    long_grad, near_zero, near_one = long_tile(
        mixed_blocks, grad_blocks, rates_local, residues_local, after_zero, after_one
    )
    grad_seq = (long_grad.reshape(local_channels, -1) + skips_local[:, None] * grads_wide).astype(
        jnp.bfloat16
    )
    skip_part = jnp.sum(grads_wide * mixed_seq.astype(jnp.float32), axis=1)
    grad_mixed = lax.all_to_all(grad_seq, "ctx", split_axis=1, concat_axis=0, tiled=True)
    first_moment, second_moment, skip_total = (
        lax.all_gather(near_zero, "ctx", axis=0, tiled=True),
        lax.all_gather(near_one, "ctx", axis=0, tiled=True),
        lax.all_gather(skip_part, "ctx", axis=0, tiled=True),
    )
    ahead_rows = passed_along(grad_mixed[:, :tap_count], "ctx", -1)
    back_window = pair_blocks(jnp.concatenate([grad_mixed, ahead_rows], axis=1), groups, tap_count)
    flipped = jnp.concatenate(
        [
            jnp.swapaxes(tap_matrix[:, :, tap_count:], 1, 2),
            jnp.swapaxes(tap_matrix[:, :, :tap_count], 1, 2),
        ],
        axis=2,
    )
    input_grad = jnp.einsum(
        "gji,gcsi->gcsj", flipped, back_window, preferred_element_type=jnp.float32
    ).reshape(channels, tokens)
    grad_sub = grad_mixed.reshape(groups, group_width, tokens // tap_count, tap_count)
    tap_pairs = jnp.einsum("gcsi,gcsj->gij", grad_sub, window, preferred_element_type=jnp.float32)
    tap_grad = jnp.einsum(
        "gij,kij->gk", tap_pairs, onehot.astype(jnp.float32), precision=top_precision
    )
    pulled = input_grad * norm_gain[:, None]
    gain_part = jnp.sum(input_grad * normed, axis=1)
    row_dot = lax.psum(jnp.sum(pulled * normed, axis=0), "ch")
    grad_inv_rms = row_dot / inverse_rms * full_width ** (-0.5)
    grad_hidden = (inverse_rms[None, :] * (pulled - normed * row_dot[None, :] / full_width)).astype(
        jnp.bfloat16
    )
    tap_total, gain_total = lax.psum((tap_grad, gain_part), "ctx")
    root_rate = jnp.sqrt(2.0 * decay_rate)
    grad_residue = root_rate * first_moment * grad_scale
    grad_log_rate = (
        residue * root_rate * (0.5 * first_moment - decay_rate * second_moment) * grad_scale
    )
    return (
        grad_hidden,
        gain_total * grad_scale,
        tap_total * grad_scale,
        grad_residue,
        grad_log_rate,
        skip_total * grad_scale,
        grad_inv_rms,
    )


def solution(mesh):
    return jax.shard_map(
        local,
        mesh=mesh,
        in_specs=(
            P("ch", "ctx"),
            P("ch", "ctx"),
            P("ch"),
            P("ch", None),
            P("ch", None),
            P("ch", None),
            P("ch"),
        ),
        out_specs=(
            P("ch", "ctx"),
            P("ch"),
            P("ch", None),
            P("ch", None),
            P("ch", None),
            P("ch"),
            P("ctx"),
        ),
        check_vma=False,
    )
```

profile of v0, /device:TPU:0, one launch (start us, length us, event | category | flops | bytes accessed | tf_op | source)
XLA Modules:
  0.0 594.5 jit_solution(8847994451295140684)
XLA Ops:
  14.7 16.7 %fusion.101 = f32[16,512,512]{2,1,0:T(8,128)} fusion(f32[16,16]{1,0:T(8,128)S(1)} %copy.81, f32[16,16]{1,0:T(8,128)S(1)} %copy.80, f32[16,16]{1,0:T(8,128)S(1)} %copy.79), kind=kOutput, calls=%fused_computation.110 | convolution fusion | flops 805699584 | bytes 16780288 | tf_op jit(solution)/shard_map/gni,gnj->gij/dot_general | solution.py:68
  31.4 30.4 %all-to-all-done = bf16[8,256,1024]{2,1,0:T(8,128)(2,1)} async-done(((bf16[8,256,1024]{2,1,0:T(8,128)(2,1)}), bf16[8,256,1024]{2,1,0:T(8,128)(2,1)}, u32[]{:S(2)}, u32[]{:S(2)}) %all-to-all-start) | async-done | bytes 4194336 | tf_op jit(solution)/shard_map/all_to_all | solution.py:121
  75.3 16.8 %convolution_bitcast_fusion.2 = f32[16,16,16,16]{1,2,3,0:T(8,128)S(1)} fusion(bf16[16,16,16,512]{3,2,1,0:T(8,128)(2,1)} %reshape.161, f32[16,16]{1,0:T(8,128)S(1)} %copy.80), kind=kOutput, calls=%fused_computation.75 | convolution fusion | flops 402784256 | bytes 4457472 | tf_op jit(solution)/shard_map/gnj,gcbj->gbnc/dot_general | solution.py:35
  92.2 15.8 %fusion = f32[16,512,16,16]{1,3,2,0:T(8,128)} fusion(bf16[16,16,16,512]{3,2,1,0:T(8,128)(2,1)S(1)} %copy-done.4, f32[16,512,512]{2,1,0:T(8,128)} %fusion.101, pred[512,512]{1,0:T(8,128)(4,1)S(1)} %iota_compare_fusion.4), kind=kOutput, calls=%fused_computation.1 | convolution fusion | flops 12889096192 | bytes 29622272 | tf_op jit(solution)/shard_map/gij,gcbi->gcbj/dot_general | solution.py:73
  112.2 11.0 %bitcast_add_fusion = f32[16,16,16,512]{3,2,1,0:T(8,128)} fusion(f32[16,512,16,16]{1,3,2,0:T(8,128)} %fusion, f32[16,16,16,16]{1,3,2,0:T(8,128)S(1)} %bitcast_add_fusion.2, f32[512]{0:T(512)S(1)} %iota_subtract_fusion.2, f32[16,16]{1,0:T(8,128)S(1)} %copy.80, f32[16,16]{1,0:T(8,128)S(1)} %copy.79), kind=kOutput, calls=%fused_computation.39 | convolution fusion | flops 405012480 | bytes 17043456 | tf_op jit(solution)/shard_map/gnj,gbnc->gcbj/dot_general | solution.py:74
  123.2 10.3 %reshape.162 = f32[256,8,1024]{2,1,0:T(8,128)} reshape(f32[16,16,16,512]{3,2,1,0:T(8,128)} %bitcast_add_fusion) | data formatting | bytes 16777216 | tf_op jit(solution)/shard_map/reshape | solution.py:144
  133.5 11.5 %fusion.22 = bf16[256,8,1024]{2,0,1:T(8,128)(2,1)} fusion(f32[256,8,1024]{2,1,0:T(8,128)} %reshape.162, f32[256]{0:T(256)S(1)} %dynamic_slice.11, bf16[8,256,1024]{2,1,0:T(8,128)(2,1)} %all-to-all-done), kind=kLoop, calls=%fused_computation.29 | loop fusion | flops 8388608 | bytes 16778240 | tf_op jit(solution)/shard_map/convert_element_type | solution.py:144
  158.6 7.4 %maximum_bitcast_fusion = bf16[128,128,256,1]{0,1,2,3:T(8,128)(2,1)} fusion(bf16[128,128,128]{0,1,2:T(8,128)(2,1)} %get-tuple-element.23, bf16[128,128,128]{0,1,2:T(8,128)(2,1)} %get-tuple-element.22), kind=kLoop, calls=%fused_computation.37 | loop fusion | flops 4194304 | bytes 16777216 | tf_op jit(solution)/shard_map/concatenate | solution.py:156
  166.0 13.5 %copy.105 = bf16[128,128,256,1]{2,1,3,0:T(8,128)(2,1)} copy(bf16[128,128,256,1]{0,1,2,3:T(8,128)(2,1)} %maximum_bitcast_fusion) | data formatting | bytes 16777216 | tf_op jit(solution)/shard_map/concatenate | solution.py:156
  179.4 19.4 %all-to-all-done.1 = bf16[256,8,1024]{2,0,1:T(8,128)(2,1)} async-done(((bf16[256,8,1024]{2,0,1:T(8,128)(2,1)}), bf16[256,8,1024]{2,0,1:T(8,128)(2,1)}, u32[]{:S(2)}, u32[]{:S(2)}) %all-to-all-start.1) | async-done | bytes 4194336 | tf_op jit(solution)/shard_map/all_to_all | solution.py:148
  205.1 12.7 %psum.28 = f32[1024]{0:T(1024)S(1)} all-reduce(f32[1024]{0:T(1024)S(1)} %fusion.20), channel_id=1, replica_groups=mesh['ctx'=8,'ch'=4] {'ch'}, use_global_device_ids=true, to_apply=%region_1.0 | all-reduce | flops 1024 | bytes 8192 | tf_op jit(solution)/shard_map/psum | solution.py:107
  222.7 10.6 %reshape.163 = bf16[128,16,9,128]{3,2,1,0:T(8,128)(2,1)} reshape(bf16[2048,1152]{1,0:T(8,128)(2,1)} %pad_maximum_fusion.3) | data formatting | bytes 9437184 | tf_op jit(solution)/shard_map/reshape | solution.py:29
  233.3 7.7 %fusion.129 = (bf16[128,16,8,128]{3,2,1,0:T(8,128)(2,1)}, bf16[128,16,8,128]{3,2,1,0:T(8,128)(2,1)}) fusion(bf16[128,16,9,128]{3,2,1,0:T(8,128)(2,1)} %reshape.163), kind=kLoop, calls=%fused_computation.158 | loop fusion | bytes 16777216 | tf_op jit(solution)/shard_map/slice | solution.py:30
  241.0 12.9 %fusion.26 = f32[128,16,8,128]{3,2,1,0:T(8,128)} fusion(bf16[128,128,256,1]{2,1,3,0:T(8,128)(2,1)} %copy.105, bf16[128,16,8,128]{3,2,1,0:T(8,128)(2,1)} %get-tuple-element.21, bf16[128,16,8,128]{3,2,1,0:T(8,128)(2,1)} %get-tuple-element.20), kind=kOutput, calls=%fused_computation.33 | convolution fusion | flops 1090519040 | bytes 25165824 | tf_op jit(solution)/shard_map/gji,gcsi->gcsj/dot_general | solution.py:163
  264.8 12.3 %copy.107 = bf16[128,128,256,1]{2,1,3,0:T(8,128)(2,1)} copy(bf16[128,128,256,1]{0,2,1,3:T(8,128)(2,1)} %bitcast.148) | data formatting | bytes 16777216 | tf_op jit(solution)/shard_map/convert_element_type | solution.py:23
  283.6 10.5 %reshape.166 = bf16[128,16,9,128]{3,2,1,0:T(8,128)(2,1)} reshape(bf16[2048,1152]{1,0:T(8,128)(2,1)} %pad_maximum_fusion.4) | data formatting | bytes 9437184 | tf_op jit(solution)/shard_map/reshape | solution.py:29
  302.9 11.4 %fusion.44 = bf16[128,16,8,128]{3,2,1,0:T(8,128)(2,1)} fusion(bf16[128,128,256,1]{2,1,3,0:T(8,128)(2,1)} %copy.107, bf16[128,16,8,128]{3,2,1,0:T(8,128)(2,1)} %get-tuple-element.19, bf16[128,16,8,128]{3,2,1,0:T(8,128)(2,1)S(1)} %get-tuple-element.18), kind=kOutput, calls=%fused_computation.56 | convolution fusion | flops 1092616192 | bytes 20971520 | tf_op jit(solution)/shard_map/gij,gcsj->gcsi/dot_general | solution.py:115
  314.3 7.4 %all_to_all.42 = bf16[8,256,1024]{2,1,0:T(8,128)(2,1)} reshape(bf16[128,16,8,128]{3,2,1,0:T(8,128)(2,1)} %fusion.44) | data formatting | bytes 8388608 | tf_op jit(solution)/shard_map/all_to_all | solution.py:120
  327.0 16.9 %convolution_bitcast_fusion.1 = f32[16,16,16,16]{1,2,3,0:T(8,128)S(1)} fusion(bf16[16,16,16,512]{3,2,1,0:T(8,128)(2,1)} %reshape.161, f32[16,16]{1,0:T(8,128)S(1)} %copy.80), kind=kOutput, calls=%fused_computation.74 | convolution fusion | flops 402915328 | bytes 4457472 | tf_op jit(solution)/shard_map/gnj,gcbj->gbnc/dot_general | solution.py:36
  354.7 8.3 %psum.29 = f32[1024]{0:T(1024)S(1)} all-reduce(f32[1024]{0:T(1024)S(1)} %copy-done.28), channel_id=1, replica_groups=mesh['ctx'=8,'ch'=4] {'ch'}, use_global_device_ids=true, to_apply=%region_3.4 | all-reduce | flops 1024 | bytes 8192 | tf_op jit(solution)/shard_map/psum | solution.py:173
  363.0 19.7 %psum.30 = f32[2048]{0:T(1024)S(1)} all-reduce(f32[2048]{0:T(1024)S(1)} %copy-done.23), channel_id=1, replica_groups=mesh['ctx'=8,'ch'=4] {'ctx'}, use_global_device_ids=true, to_apply=%region_5.6 | all-reduce | flops 2048 | bytes 16384 | tf_op jit(solution)/shard_map/psum | solution.py:178
  383.3 8.7 %fusion.17 = bf16[2048,1024]{1,0:T(8,128)(2,1)} fusion(bf16[2048,1024]{1,0:T(8,128)(2,1)} %param.7, f32[256,8,8,128]{3,2,1,0:T(8,128)} %bitcast.150, f32[1024]{0:T(1024)S(1)} %psum.29, f32[2048]{0:T(1024)S(1)} %copy-done.18, f32[1024]{0:T(1024)S(1)} %add_rsqrt_fusion), kind=kLoop, calls=%fused_computation.24 | loop fusion | flops 16777216 | bytes 16793600 | tf_op jit(solution)/shard_map/convert_element_type | solution.py:175
  392.0 12.8 %convolution_bitcast_fusion = f32[128,128,256]{2,1,0:T(8,128)} fusion(bf16[128,16,8,128]{3,2,1,0:T(8,128)(2,1)} %get-tuple-element.19, bf16[128,16,8,128]{3,2,1,0:T(8,128)(2,1)} %copy-done.11, bf16[128,16,8,128]{3,2,1,0:T(8,128)(2,1)} %bitcast.151), kind=kOutput, calls=%fused_computation.19 | convolution fusion | flops 1090519040 | bytes 29360128 | tf_op jit(solution)/shard_map/gcsi,gcsj->gij/dot_general | solution.py:167
  404.8 22.6 %fusion.75 = f32[128,128]{1,0:T(8,128)} fusion(s32[128,256]{1,0:T(8,128)S(1)} %iota_subtract_fusion.1, f32[128,128,256]{2,1,0:T(8,128)} %convolution_bitcast_fusion), kind=kOutput, calls=%fused_computation.82 | convolution fusion | flops 6446645248 | bytes 16973824 | tf_op jit(solution)/shard_map/gij,kij->gk/dot_general | solution.py:168
  428.0 49.6 %all-reduce.2.cloned.1.call-done = f32[128,128]{1,0:T(8,128)} async-done(((f32[128,128]{1,0:T(8,128)}), f32[128,128]{1,0:T(8,128)}) %all-reduce.2.cloned.1.call-update) | async-done | bytes 65552 | tf_op jit(solution)/shard_map/psum | solution.py:178
  492.7 11.7 %fusion.130 = f32[16,512,512,1]{1,2,3,0:T(8,128)} fusion(bf16[16,16,16,512]{3,2,1,0:T(8,128)(2,1)} %reshape.167, bf16[16,16,16,512]{3,2,1,0:T(8,128)(2,1)} %reshape.161), kind=kOutput, calls=%fused_computation.159 | convolution fusion | flops 2147483648 | bytes 25165824 | tf_op jit(solution)/shard_map/gcbi,gcbj->gij/dot_general | solution.py:77
  514.1 13.9 %fusion.67 = f32[16,16]{1,0:T(8,128)S(1)} fusion(f32[16,512,512,1]{1,2,3,0:T(8,128)} %fusion.130, pred[512,512]{1,0:T(8,128)(4,1)S(1)} %iota_compare_fusion.4, f32[16,16]{1,0:T(8,128)S(1)} %copy-done.15, f32[16,16]{1,0:T(8,128)S(1)} %copy.80), kind=kOutput, calls=%fused_computation.80 | convolution fusion | flops 810024704 | bytes 17042432 | tf_op jit(solution)/shard_map/gni,gij,gnj->gn/dot_general | solution.py:82
  528.0 11.0 %fusion.68 = f32[16,16]{1,0:T(8,128)S(1)} fusion(f32[16,512,512,1]{1,2,3,0:T(8,128)S(1)} %copy-done.2, f32[512,512]{1,0:T(8,128)S(1)} %copy-done.12, pred[512,512]{1,0:T(8,128)(4,1)S(1)} %iota_compare_fusion.4, f32[16,16]{1,0:T(8,128)S(1)} %copy-done.15, f32[16,16]{1,0:T(8,128)S(1)} %copy.80), kind=kOutput, calls=%fused_computation.81 | convolution fusion | flops 814219008 | bytes 18091008 | tf_op jit(solution)/shard_map/gni,gij,gnj->gn/dot_general | solution.py:83
  548.1 7.4 %fusion.47 = f32[16,16]{1,0:T(8,128)S(1)} fusion(f32[16,16,16,16]{1,3,2,0:T(8,128)S(1)} %bitcast_add_fusion.2, f32[16,16,16,16]{2,1,3,0:T(8,128)} %copy.97, f32[16,16,16,16]{2,1,3,0:T(8,128)S(1)} %copy-done.10, f32[16,16,16,16]{3,2,1,0:T(8,128)} %fusion.49, f32[16,16,16,16]{1,2,3,0:T(8,128)S(1)} %copy-done.9, f32[16]{0:T(128)S(1)} %copy-done.29, ...), kind=kOutput, calls=%fused_computation.60 | convolution fusion | flops 13238016 | bytes 1330496 | tf_op jit(solution)/shard_map/gnbk,gknc->gbnc/dot_general | solution.py:50
  555.4 8.6 %all_gather.10 = f32[128,16]{1,0:T(8,128)S(1)} all-gather(f32[16,16]{1,0:T(8,128)S(1)} %add.84), channel_id=1, replica_groups=mesh['ctx'=8,'ch'=4] {'ctx'}, dimensions={0}, use_global_device_ids=true | all-gather | bytes 9216 | tf_op jit(solution)/shard_map/all_gather | solution.py:151
  564.1 8.9 %all_gather.9 = f32[128,16]{1,0:T(8,128)S(1)} all-gather(f32[16,16]{1,0:T(8,128)S(1)} %add.79), channel_id=1, replica_groups=mesh['ctx'=8,'ch'=4] {'ctx'}, dimensions={0}, use_global_device_ids=true | all-gather | bytes 9216 | tf_op jit(solution)/shard_map/all_gather | solution.py:150
  577.7 8.2 %all-gather = f32[8,1,256]{2,1,0:T(1,128)S(1)} all-gather(f32[1,1,256]{2,1,0:T(1,128)S(1)} %bitcast.154), channel_id=1, replica_groups=mesh['ctx'=8,'ch'=4] {'ctx'}, dimensions={0}, use_global_device_ids=true | all-gather | bytes 9216 | tf_op jit(solution)/shard_map/all_gather | solution.py:152
  (118 shorter events, 133.1 us)
Async XLA Ops:
  7.2 142.6 %copy-start = (bf16[128,128]{1,0:T(8,128)(2,1)S(1)}, bf16[128,128]{1,0:T(8,128)(2,1)}, u32[]{:S(2)}) copy-start(bf16[128,128]{1,0:T(8,128)(2,1)} %param.10) | copy-start | bytes 98308
  7.2 5.3 copy-start.24
  7.2 5.3 copy-start.26
  7.2 54.5 %all-to-all-start = ((bf16[8,256,1024]{2,1,0:T(8,128)(2,1)}), bf16[8,256,1024]{2,1,0:T(8,128)(2,1)}, u32[]{:S(2)}, u32[]{:S(2)}) async-start(bf16[8,256,1024]{2,1,0:T(8,128)(2,1)} %bitcast.152), calls=%async_computation | async-start | bytes 8388608 | tf_op jit(solution)/shard_map/all_to_all | solution.py:121
  12.7 18.7 %copy-start.14 = (f32[16,16]{1,0:T(8,128)}, f32[16,16]{1,0:T(8,128)S(1)}, u32[]{:S(2)}) copy-start(f32[16,16]{1,0:T(8,128)S(1)} %copy.81) | copy-start | bytes 3076
  13.6 94.4 %copy-start.19 = (pred[16,16]{1,0:T(8,128)(4,1)}, pred[16,16]{1,0:T(8,128)(4,1)S(1)}, u32[]{:S(2)}) copy-start(pred[16,16]{1,0:T(8,128)(4,1)S(1)} %fusion.118) | copy-start | bytes 772
  13.6 98.5 %copy-start.21 = (f32[512]{0:T(512)}, f32[512]{0:T(512)S(1)}, u32[]{:S(2)}) copy-start(f32[512]{0:T(512)S(1)} %iota_subtract_fusion.2) | copy-start | bytes 6148
  13.7 94.4 %copy-start.16 = (f32[16,16]{1,0:T(8,128)}, f32[16,16]{1,0:T(8,128)S(1)}, u32[]{:S(2)}) copy-start(f32[16,16]{1,0:T(8,128)S(1)} %multiply_convert_fusion) | copy-start | bytes 3076
  75.3 16.8 %copy-start.4 = (bf16[16,16,16,512]{3,2,1,0:T(8,128)(2,1)S(1)}, bf16[16,16,16,512]{3,2,1,0:T(8,128)(2,1)}, u32[]{:S(2)}) copy-start(bf16[16,16,16,512]{3,2,1,0:T(8,128)(2,1)} %reshape.161) | copy-start | bytes 12582916
  92.2 15.9 %copy-start.8 = (f32[16,16,16,16]{1,2,3,0:T(8,128)}, f32[16,16,16,16]{1,2,3,0:T(8,128)S(1)}, u32[]{:S(2)}) copy-start(f32[16,16,16,16]{1,2,3,0:T(8,128)S(1)} %convolution_bitcast_fusion.2) | copy-start | bytes 786436
  145.1 53.7 %all-to-all-start.1 = ((bf16[256,8,1024]{2,0,1:T(8,128)(2,1)}), bf16[256,8,1024]{2,0,1:T(8,128)(2,1)}, u32[]{:S(2)}, u32[]{:S(2)}) async-start(bf16[256,8,1024]{2,0,1:T(8,128)(2,1)} %fusion.22), calls=%async_computation.1 | async-start | bytes 8388608 | tf_op jit(solution)/shard_map/all_to_all | solution.py:148
  152.4 6.1 %copy-start.3 = (bf16[128,256,128]{2,1,0:T(8,128)(2,1)}, bf16[128,256,128]{2,1,0:T(8,128)(2,1)S(1)}, u32[]{:S(2)}) copy-start(bf16[128,256,128]{2,1,0:T(8,128)(2,1)S(1)} %fusion.39) | copy-start | bytes 25165828
  200.7 17.2 %collective-permute-start = (bf16[2048,128]{1,0:T(8,128)(2,1)}, bf16[2048,128]{1,0:T(8,128)(2,1)S(1)}, u32[]{:S(2)}, u32[]{:S(2)}) collective-permute-start(bf16[2048,128]{1,0:T(8,128)(2,1)} %slice.32), channel_id=1, source_target_pairs={{4,0},{8,4},{12,8},{16,12},{20,16},{24,20},{28,24},{5,1},{9,5},{13... | collective-permute-start | bytes 1572872 | tf_op jit(solution)/shard_map/ppermute | solution.py:13
  241.0 12.9 %copy-start.6 = (bf16[2048,1024]{1,0:T(8,128)(2,1)S(1)}, bf16[2048,1024]{1,0:T(8,128)(2,1)}, u32[]{:S(2)}) copy-start(bf16[2048,1024]{1,0:T(8,128)(2,1)} %param.7) | copy-start | bytes 12582916
  241.0 12.9 %copy-start.18 = (f32[2048]{0:T(1024)S(1)}, f32[2048]{0:T(1024)}, u32[]{:S(2)}) copy-start(f32[2048]{0:T(1024)} %param.9) | copy-start | bytes 24580
  263.5 15.3 %collective-permute-start.1 = (bf16[2048,128]{1,0:T(8,128)(2,1)}, bf16[2048,128]{1,0:T(8,128)(2,1)S(1)}, u32[]{:S(2)}, u32[]{:S(2)}) collective-permute-start(bf16[2048,128]{1,0:T(8,128)(2,1)} %slice.37), channel_id=1, source_target_pairs={{0,4},{4,8},{8,12},{12,16},{16,20},{20,24},{24,28},{1,5},{5,9},{9,... | collective-permute-start | bytes 1572872 | tf_op jit(solution)/shard_map/ppermute | solution.py:13
  321.7 157.4 %all-to-all-start.2 = ((bf16[8,256,1024]{2,1,0:T(8,128)(2,1)}), bf16[8,256,1024]{2,1,0:T(8,128)(2,1)}, u32[]{:S(2)}, u32[]{:S(2)}) async-start(bf16[8,256,1024]{2,1,0:T(8,128)(2,1)} %all_to_all.42), calls=%async_computation.2 | async-start | bytes 8388608 | tf_op jit(solution)/shard_map/all_to_all | solution.py:120
  327.0 17.0 %copy-start.17 = (f32[16,16]{1,0:T(8,128)S(1)}, f32[16,16]{1,0:T(8,128)}, u32[]{:S(2)}) copy-start(f32[16,16]{1,0:T(8,128)} %copy-done.16) | copy-start | bytes 3076
  327.0 17.0 %copy-start.20 = (pred[16,16]{1,0:T(8,128)(4,1)S(1)}, pred[16,16]{1,0:T(8,128)(4,1)}, u32[]{:S(2)}) copy-start(pred[16,16]{1,0:T(8,128)(4,1)} %copy-done.19) | copy-start | bytes 772
  327.0 150.6 %all-reduce.2.cloned.1.call-start = ((), (), s32[]{:S(2)}) async-start(), calls=%async_computation.3 | async-start | bytes 131072 | tf_op jit(solution)/shard_map/psum | solution.py:178
  349.4 5.3 copy-start.28
  349.4 13.6 %copy-start.23 = (f32[2048]{0:T(1024)S(1)}, f32[2048]{0:T(1024)}, u32[]{:S(2)}) copy-start(f32[2048]{0:T(1024)} %get-tuple-element.14) | copy-start | bytes 24580
  492.7 11.7 %copy-start.5 = (bf16[16,16,16,512]{3,2,1,0:T(8,128)(2,1)S(1)}, bf16[16,16,16,512]{3,2,1,0:T(8,128)(2,1)}, u32[]{:S(2)}) copy-start(bf16[16,16,16,512]{3,2,1,0:T(8,128)(2,1)} %reshape.167) | copy-start | bytes 12582916
  492.7 11.7 %copy-start.22 = (f32[512]{0:T(512)S(1)}, f32[512]{0:T(512)}, u32[]{:S(2)}) copy-start(f32[512]{0:T(512)} %copy-done.21) | copy-start | bytes 6148
  509.2 4.8 copy-start.15
  509.3 18.7 %copy-start.12 = (f32[512,512]{1,0:T(8,128)S(1)}, f32[512,512]{1,0:T(8,128)}, u32[]{:S(2)}) copy-start(f32[512,512]{1,0:T(8,128)} %iota_subtract_fusion) | copy-start | bytes 3145732
  514.1 13.9 %copy-start.2 = (f32[16,512,512,1]{1,2,3,0:T(8,128)S(1)}, f32[16,512,512,1]{1,2,3,0:T(8,128)}, u32[]{:S(2)}) copy-start(f32[16,512,512,1]{1,2,3,0:T(8,128)} %fusion.130) | copy-start | bytes 50331652
  542.0 5.7 copy-start.13
  542.0 5.7 copy-start.29
  573.0 14.2 %copy-start.1 = (bf16[128,128]{1,0:T(8,128)(2,1)S(1)}, bf16[128,128]{1,0:T(8,128)(2,1)}, u32[]{:S(2)}) copy-start(bf16[128,128]{1,0:T(8,128)(2,1)} %param.10) | copy-start | bytes 98308
  573.0 13.5 %copy-start.25 = (f32[128,16]{0,1:T(8,128)S(1)}, f32[128,16]{0,1:T(8,128)}, u32[]{:S(2)}) copy-start(f32[128,16]{0,1:T(8,128)} %param.11) | copy-start | bytes 24580
  573.0 13.5 %copy-start.27 = (f32[128,16]{0,1:T(8,128)S(1)}, f32[128,16]{0,1:T(8,128)}, u32[]{:S(2)}) copy-start(f32[128,16]{0,1:T(8,128)} %param.12) | copy-start | bytes 24580
  (4 other events, 9.3 us)
Sparse Core Ops, SparseCore 0:
  427.5 50.0 all-reduce.1
where the time goes:
time: 605 us; the launch traced here: 594 us
  matrix products  203 us (34%)
  local copies, waits for them, and re-layouts  132 us (22%)
  waiting for transfers between devices  99.4 us (16%)
  blocking collectives  66.5 us (11%)
  other arithmetic  60.8 us (10%)
  starting transfers between devices  17.8 us (3%)
  between operations  14.8 us (2%)
    psum x1, waiting for transfers between devices, local(): tap_total, gain_total = lax.psum((tap_grad, gain_part), 'ctx')  49.6 us
    all_to_all x1, waiting for transfers between devices, local(): lax.all_to_all(cotangent, 'ctx', split_axis=0, concat_axis=1, tiled=True)  30.4 us
    dot_general x1, matrix products, local(): jnp.einsum('gij,kij->gk', tap_pairs, onehot.astype(jnp.float32), precisio...  22.6 us
    reshape x2, local copies, waits for them, and re-layouts, pair_blocks(): joined.reshape(groups, channels // groups, joined.shape[1] // tap_count,...  21.1 us
    psum x1, blocking collectives, local(): tap_total, gain_total = lax.psum((tap_grad, gain_part), 'ctx')  19.7 us
    all_to_all x1, waiting for transfers between devices, local(): lax.all_to_all(grad_seq, 'ctx', split_axis=1, concat_axis=0, tiled=True)  19.4 us
    dot_general x1, matrix products, block_states(): jnp.einsum('gnj,gcbj->gbnc', falling * steps, grads_wide, precision=top_p...  16.9 us
    dot_general x1, matrix products, block_states(): jnp.einsum('gnj,gcbj->gbnc', falling, grads_wide, precision=top_precision)  16.8 us
  transfers between devices with their start and end apart: 6, of which 3 were waited for; matrix products, arithmetic and copies ran while one was open for 23% of the time, Pallas kernels for 0%

commit v1 on v0

v1 whole, which is shorter than its diff:
```python
import functools

import jax
import jax.numpy as jnp
from jax import lax
from jax.experimental import pallas as pl
from jax.experimental.pallas import tpu as pltpu
from jax.sharding import PartitionSpec as P

eps_norm = 1e-06
W = 128
GW = 16
PACK = W // GW
VMEM_LIMIT = 48 * 1024 * 1024


def passed_along(x, axis, by):
    count = lax.axis_size(axis)
    pairs = [(i, i + by) for i in range(count) if 0 <= i + by < count]
    return lax.ppermute(x, axis, pairs)


def dot(a, b, ca, cb):
    return lax.dot_general(
        a, b, (((ca,), (cb,)), ((), ())), preferred_element_type=jnp.float32
    )


def columns_of(row):
    return jnp.broadcast_to(row, (W, W)).T


def row_sums(stack):
    return jnp.sum(stack.T, axis=0, keepdims=True)


def split_two(x):
    high = x.astype(jnp.bfloat16)
    return high, (x - high.astype(jnp.float32)).astype(jnp.bfloat16)


def circulant(row):
    return pltpu.roll(jnp.broadcast_to(row, (W, W)), 0, 1, stride=1, stride_axis=0)


def diagonal_sums(x):
    half = W // 2
    while half >= 8:
        x = x[:half] + pltpu.roll(x[half:], W - half, 1)
        half //= 2
    for by in (4, 2, 1):
        x = x + pltpu.roll(pltpu.roll(x, W - by, 1), 8 - by, 0)
    return x[:1]


def tiles_of(ref, rows, blocks):
    return [ref[rows, W * k : W * (k + 1)] for k in range(blocks)]


def state_kernel(rate_ref, g_ref, ga_ref, s0_ref, s1_ref, total_ref):
    blocks = g_ref.shape[1] // W
    rates = columns_of(rate_ref[0])
    lane_int = lax.broadcasted_iota(jnp.int32, (GW, W), 1)
    lane = lane_int.astype(jnp.float32)
    seg = lane_int // GW
    total0 = jnp.zeros((GW, W), jnp.float32)
    total1 = jnp.zeros((GW, W), jnp.float32)
    for q in range(PACK):
        rows = slice(GW * q, GW * (q + 1))
        r = rates[rows]
        fall = jnp.exp(-r * lane)
        table = jnp.concatenate(split_two(fall) + split_two(fall * lane), axis=0)
        data = jnp.concatenate(tiles_of(g_ref, rows, blocks)[1:] + [ga_ref[rows, :]], axis=0)
        sums = dot(table, data, 1, 1)
        s0 = sums[:GW] + sums[GW : 2 * GW]
        s1 = sums[2 * GW : 3 * GW] + sums[3 * GW :]
        by = 1
        while by < blocks:
            decay = jnp.exp(-r * float(W * by))
            keep = seg + by < blocks
            a0 = jnp.where(keep, pltpu.roll(s0, W - GW * by, 1), 0.0)
            a1 = jnp.where(keep, pltpu.roll(s1, W - GW * by, 1), 0.0)
            s1 = s1 + decay * (a1 + float(W * by) * a0)
            s0 = s0 + decay * a0
            by *= 2
        s0_ref[q] = s0
        s1_ref[q] = s1
        here = seg == q
        total0 = jnp.where(here, pltpu.roll(s0, GW * q, 1) if q else s0, total0)
        total1 = jnp.where(here, pltpu.roll(s1, GW * q, 1) if q else s1, total1)
    total_ref[0, :GW] = total0
    total_ref[0, GW:] = total1


def main_kernel(
    rank_ref, rate_ref, res_ref, gain_ref, skip_ref, tap_ref, inv_ref, h_ref, hb_ref, g_ref, ga_ref,
    s0_ref, s1_ref, total_ref,
    ig_ref, tapg_ref, mom0_ref, mom1_ref, skipg_ref, gaing_ref, dot_ref,
):
    tokens = g_ref.shape[1]
    blocks = tokens // W
    count = total_ref.shape[0]
    rank = rank_ref[0]
    rates = columns_of(rate_ref[0])
    residues = columns_of(res_ref[0])
    gains = columns_of(gain_ref[0])
    skips = columns_of(skip_ref[0])
    lane_int = lax.broadcasted_iota(jnp.int32, (GW, W), 1)
    lane = lane_int.astype(jnp.float32)
    seg = lane_int // GW
    upper = lax.broadcasted_iota(jnp.int32, (W, W), 1) >= lax.broadcasted_iota(
        jnp.int32, (W, W), 0
    )
    rate_seg = jnp.zeros((GW, W), jnp.float32)
    for q in range(PACK):
        rate_seg = jnp.where(seg == q, rates[GW * q : GW * (q + 1)], rate_seg)
    in0 = jnp.zeros((GW, W), jnp.float32)
    in1 = jnp.zeros((GW, W), jnp.float32)
    for m in range(1, count):
        gap = m - rank - 1
        span = (jnp.maximum(gap, 0) * tokens).astype(jnp.float32)
        factor = jnp.where(gap >= 0, jnp.exp(-rate_seg * span), 0.0)
        t0 = total_ref[m, 0, :GW]
        in0 = in0 + factor * t0
        in1 = in1 + factor * (total_ref[m, 0, GW:] + span * t0)
    left = ((blocks - seg) * W).astype(jnp.float32)

    @pl.when(pl.program_id(0) == 0)
    def _():
        dot_ref[...] = jnp.zeros_like(dot_ref)

    inv_back = inv_ref[:, :W]
    inv = [inv_ref[:, W * (k + 1) : W * (k + 2)] for k in range(blocks)]
    moments0, moments1, skip_rows, gain_rows = [], [], [], []
    dots = None
    for q in range(PACK):
        rows = slice(GW * q, GW * (q + 1))
        r = rates[rows]
        amp = residues[rows] * jnp.sqrt(2.0 * r)
        gain = gains[rows]
        skip = skips[rows]
        fall = jnp.exp(-r * lane)
        kern = jnp.sum(amp * fall, axis=0, keepdims=True)
        kern_high, kern_low = split_two(jnp.where(upper, circulant(kern), 0.0))
        circ = circulant(tap_ref[q : q + 1, :])
        now = jnp.where(upper, circ, 0.0).astype(jnp.bfloat16)
        before = jnp.where(upper, 0.0, circ).astype(jnp.bfloat16)
        normed = [t.astype(jnp.float32) * i for t, i in zip(tiles_of(h_ref, rows, blocks), inv)]
        units = [(n * gain).astype(jnp.bfloat16) for n in normed]
        unit_back = (hb_ref[rows, :].astype(jnp.float32) * inv_back * gain).astype(jnp.bfloat16)
        x_now = jnp.concatenate(units, axis=0)
        x_before = jnp.concatenate([unit_back] + units[:-1], axis=0)
        mixed = (dot(x_now, now, 1, 0) + dot(x_before, before, 1, 0)).astype(jnp.bfloat16)
        g_tiles = tiles_of(g_ref, rows, blocks)
        grads = jnp.concatenate(g_tiles, axis=0)
        grads_long = jnp.concatenate(g_tiles + [ga_ref[rows, :]], axis=0)
        a0in = jnp.where(seg == q, in0, 0.0)
        a1in = jnp.where(seg == q, in1, 0.0)
        for by in (GW, 2 * GW, 4 * GW):
            a0in = a0in + pltpu.roll(a0in, by, 1)
            a1in = a1in + pltpu.roll(a1in, by, 1)
        decay = jnp.exp(-r * left)
        after0 = s0_ref[q] + decay * a0in
        after1 = s1_ref[q] + decay * (a1in + left * a0in)
        gap = float(W) - lane
        to_end = jnp.exp(-r * gap)
        a_high, a_low = split_two(jnp.concatenate([after0, a0in], axis=1))
        w_high, w_low = split_two(amp * to_end)
        outer = dot(
            jnp.concatenate([a_high, a_low, a_high], axis=0),
            jnp.concatenate([w_high, w_high, w_low], axis=0),
            0, 0,
        )[: W + GW]
        wide = grads_long.astype(jnp.float32)
        gm = (
            dot(grads_long, kern_high, 1, 1)
            + dot(grads_long, kern_low, 1, 1)
            + outer
            + jnp.concatenate([skip] * (blocks + 1), axis=0) * wide
        ).astype(jnp.bfloat16)
        gm_now = gm[:W]
        ig = dot(gm_now, now, 1, 1) + dot(gm[GW:], before, 1, 1)
        pairs = jnp.where(upper, dot(x_now, gm_now, 0, 0), dot(x_before, gm_now, 0, 0))
        tapg_ref[q : q + 1, :] = diagonal_sums(pairs)
        lags = diagonal_sums(jnp.where(upper, dot(mixed, grads, 0, 0), 0.0))
        table = jnp.concatenate(split_two(to_end) + split_two(to_end * gap), axis=0)
        lifted = dot(table, mixed, 1, 1)
        l0 = lifted[:GW] + lifted[GW : 2 * GW]
        l1 = lifted[2 * GW : 3 * GW] + lifted[3 * GW :]
        near = lags * fall
        moments0.append(l0 * after0 + near)
        moments1.append(l1 * after0 + l0 * after1 + near * lane)
        skip_terms = wide[:W] * mixed.astype(jnp.float32)
        gain_terms = ig * jnp.concatenate(normed, axis=0)
        skip_sum = skip_terms[:GW]
        gain_sum = gain_terms[:GW]
        for k in range(blocks):
            part = slice(GW * k, GW * (k + 1))
            ig_ref[rows, W * k : W * (k + 1)] = ig[part]
            if k:
                skip_sum = skip_sum + skip_terms[part]
                gain_sum = gain_sum + gain_terms[part]
        skip_rows.append(skip_sum)
        gain_rows.append(gain_sum)
        dot_ref[...] += gain_terms * jnp.concatenate([gain] * blocks, axis=0)
    mom0_ref[0] = row_sums(jnp.concatenate(moments0, axis=0))
    mom1_ref[0] = row_sums(jnp.concatenate(moments1, axis=0))
    skipg_ref[0] = row_sums(jnp.concatenate(skip_rows, axis=0))
    gaing_ref[0] = row_sums(jnp.concatenate(gain_rows, axis=0))


def local(hidden, cotangent, norm_gain, mr_filter, residue, decay_rate, skip_weight):
    channels, tokens = hidden.shape
    groups = mr_filter.shape[0]
    ctx_count = lax.axis_size("ctx")
    full_width = channels * lax.axis_size("ch")
    grad_scale = (tokens * ctx_count) ** (-0.5)
    steps = groups // PACK
    f32 = jnp.float32

    hidden_back = passed_along(hidden[:, tokens - W :], "ctx", 1)
    cot_ahead = passed_along(cotangent[:, :W], "ctx", -1)

    def squares_of(x):
        wide = x.astype(f32)
        return jnp.sum(wide * wide, axis=0)

    squares = lax.psum(
        jnp.concatenate([squares_of(hidden_back), squares_of(hidden)]), "ch"
    )
    inverse_all = lax.rsqrt(squares / full_width + eps_norm)
    inverse_rms = inverse_all[W:]

    rate_rows = decay_rate.reshape(steps, 1, W)
    residue_rows = residue.reshape(steps, 1, W)
    gain_rows = norm_gain.reshape(steps, 1, W)
    skip_rows = skip_weight.reshape(steps, 1, W)

    row_spec = pl.BlockSpec((1, 1, W), lambda i: (i, 0, 0))
    wide_spec = pl.BlockSpec((W, tokens), lambda i: (i, 0))
    edge_spec = pl.BlockSpec((W, W), lambda i: (i, 0))
    state_spec = pl.BlockSpec((PACK, GW, W), lambda i: (i, 0, 0))
    row_shape = jax.ShapeDtypeStruct((steps, 1, W), f32)
    state_shape = jax.ShapeDtypeStruct((groups, GW, W), f32)

    state0, state1, total = pl.pallas_call(
        state_kernel,
        grid=(steps,),
        in_specs=[row_spec, wide_spec, edge_spec],
        out_specs=[state_spec, state_spec, pl.BlockSpec((1, 2 * GW, W), lambda i: (i, 0, 0))],
        out_shape=[state_shape, state_shape, jax.ShapeDtypeStruct((steps, 2 * GW, W), f32)],
        compiler_params=pltpu.CompilerParams(vmem_limit_bytes=VMEM_LIMIT),
        cost_estimate=pl.CostEstimate(
            flops=groups * 2 * 64 * W * W, bytes_accessed=8 * 2**20, transcendentals=0
        ),
        name="states",
    )(rate_rows, cotangent, cot_ahead)
    totals = lax.all_gather(total, "ctx", axis=0, tiled=False)

    rank = lax.axis_index("ctx").astype(jnp.int32).reshape(1)
    input_grad, tap_part, mom0, mom1, skip_part, gain_part, dots = pl.pallas_call(
        main_kernel,
        grid=(steps,),
        in_specs=[
            pl.BlockSpec(memory_space=pltpu.SMEM),
            row_spec, row_spec, row_spec, row_spec,
            pl.BlockSpec((PACK, W), lambda i: (i, 0)),
            pl.BlockSpec((1, tokens + W), lambda i: (0, 0)),
            wide_spec, edge_spec, wide_spec, edge_spec,
            state_spec, state_spec,
            pl.BlockSpec((ctx_count, 1, 2 * GW, W), lambda i: (0, i, 0, 0)),
        ],
        out_specs=[
            wide_spec,
            pl.BlockSpec((PACK, W), lambda i: (i, 0)),
            row_spec, row_spec, row_spec, row_spec,
            pl.BlockSpec((W, W), lambda i: (0, 0)),
        ],
        out_shape=[
            jax.ShapeDtypeStruct((channels, tokens), f32),
            jax.ShapeDtypeStruct((groups, W), f32),
            row_shape, row_shape, row_shape, row_shape,
            jax.ShapeDtypeStruct((W, W), f32),
        ],
        compiler_params=pltpu.CompilerParams(vmem_limit_bytes=VMEM_LIMIT),
        cost_estimate=pl.CostEstimate(
            flops=groups * 24 * W**3, bytes_accessed=24 * 2**20, transcendentals=0
        ),
        name="main",
    )(
        rank, rate_rows, residue_rows, gain_rows, skip_rows, mr_filter.astype(f32),
        inverse_all.reshape(1, tokens + W), hidden, hidden_back, cotangent, cot_ahead,
        state0, state1, totals,
    )
    row_dot = lax.psum(
        jnp.sum(dots.reshape(tokens // W, GW, W), axis=1).reshape(tokens), "ch"
    )
    parts = jnp.concatenate(
        [tap_part] + [x.reshape(steps, W) for x in (mom0, mom1, skip_part, gain_part)], axis=0
    )
    whole = jnp.sum(lax.all_gather(parts, "ctx", axis=0, tiled=False), axis=0)
    tap_total = whole[:groups]
    first, second, skip_total, gain_total = (
        whole[groups + steps * i : groups + steps * (i + 1)] for i in range(4)
    )
    first_moment = first.reshape(decay_rate.shape)
    second_moment = second.reshape(decay_rate.shape)

    normed = hidden.astype(f32) * inverse_rms[None, :]
    pulled = input_grad * norm_gain[:, None]
    grad_inv_rms = row_dot / inverse_rms * full_width ** (-0.5)
    grad_hidden = (inverse_rms[None, :] * (pulled - normed * row_dot[None, :] / full_width)).astype(
        jnp.bfloat16
    )
    root_rate = jnp.sqrt(2.0 * decay_rate)
    grad_residue = root_rate * first_moment * grad_scale
    grad_log_rate = (
        residue * root_rate * (0.5 * first_moment - decay_rate * second_moment) * grad_scale
    )
    return (
        grad_hidden,
        gain_total.reshape(channels) * grad_scale,
        tap_total * grad_scale,
        grad_residue,
        grad_log_rate,
        skip_total.reshape(channels) * grad_scale,
        grad_inv_rms,
    )


def solution(mesh):
    return jax.shard_map(
        local,
        mesh=mesh,
        in_specs=(
            P("ch", "ctx"),
            P("ch", "ctx"),
            P("ch"),
            P("ch", None),
            P("ch", None),
            P("ch", None),
            P("ch"),
        ),
        out_specs=(
            P("ch", "ctx"),
            P("ch"),
            P("ch", None),
            P("ch", None),
            P("ch", None),
            P("ch"),
            P("ctx"),
        ),
        check_vma=False,
    )
```

time: 605 us -> 185 us (0.31); the launches traced: 594 us -> 184 us
  matrix products: 203 us -> 0 us
  local copies, waits for them, and re-layouts: 132 us -> 6.61 us
  Pallas kernels: 0 us -> 93.4 us
  waiting for transfers between devices: 99.4 us -> 10.8 us
  other arithmetic: 60.8 us -> 13.8 us
  blocking collectives: 66.5 us -> 34.2 us
  starting transfers between devices: 17.8 us -> 11.3 us
    dot_general x18 -> x0, matrix products: 203 us -> none  [the longest x1 22.6 us: local(): jnp.einsum('gij,kij->gk', tap_pairs, onehot.astype(jnp.float32), precisio...]
    pallas_call x0 -> x2, Pallas kernels: none -> 93.4 us  [the longest x1 79.5 us: local(): pl.pallas_call(main_kernel, grid=(steps,), in_specs=[pl.BlockSpec(memory_...]
    all_to_all x3 -> x0, waiting for transfers between devices: 49.7 us -> none  [the longest x1 30.4 us: local(): lax.all_to_all(cotangent, 'ctx', split_axis=0, concat_axis=1, tiled=True)]
    psum x1 -> x0, waiting for transfers between devices: 49.6 us -> none  [local(): tap_total, gain_total = lax.psum((tap_grad, gain_part), 'ctx')]
    reshape x5 -> x7, local copies, waits for them, and re-layouts: 45.6 us -> 0.44 us  [the longest x2 0.15 us: local(): first_moment = first.reshape(decay_rate.shape)]
    all_to_all x3 -> x0, local copies, waits for them, and re-layouts: 20.4 us -> none  [the longest x2 13.8 us: local(): lax.all_to_all(mixed, 'ctx', split_axis=0, concat_axis=1, tiled=True)]
    concatenate x3 -> x1, other arithmetic: 17.1 us -> 0.01 us  [local(): jnp.concatenate([squares_of(hidden_back), squares_of(hidden)])]
    psum x3 -> x2, blocking collectives: 40.8 us -> 23.8 us  [the longest x1 12.1 us: local(): lax.psum(jnp.concatenate([squares_of(hidden_back), squares_of(hidden)]),...]
  transfers between devices with their start and end apart: 6 -> 3, of which waited for: 3 -> 2; matrix products, arithmetic and copies ran while one was open for 23% -> 4% of each run, Pallas kernels for 0% -> 0%
where the time goes in v1:
time: 185 us; the launch traced here: 184 us
  Pallas kernels  93.4 us (50%)
  blocking collectives  34.2 us (18%)
  between operations  14.2 us (8%)
  other arithmetic  13.8 us (7%)
  starting transfers between devices  11.3 us (6%)
  waiting for transfers between devices  10.8 us (6%)
  local copies, waits for them, and re-layouts  6.61 us (4%)
    pallas_call x1, Pallas kernels, local(): pl.pallas_call(main_kernel, grid=(steps,), in_specs=[pl.BlockSpec(memory_...  79.5 us
    pallas_call x1, Pallas kernels, local(): pl.pallas_call(state_kernel, grid=(steps,), in_specs=[row_spec, wide_spec...  13.9 us
    psum x1, blocking collectives, local(): lax.psum(jnp.concatenate([squares_of(hidden_back), squares_of(hidden)]),...  12.1 us
    psum x1, blocking collectives, local(): lax.psum(jnp.sum(dots.reshape(tokens // W, GW, W), axis=1).reshape(tokens...  11.7 us
    ppermute x2, starting transfers between devices, passed_along(): return lax.ppermute(x, axis, pairs)  11.2 us
    all_gather x1, blocking collectives, local(): whole = jnp.sum(lax.all_gather(parts, 'ctx', axis=0, tiled=False), axis=0)  10.4 us
    all_gather x1, waiting for transfers between devices, local(): totals = lax.all_gather(total, 'ctx', axis=0, tiled=False)  9.12 us
    convert_element_type x1, other arithmetic, local(): (inverse_rms[None, :] * (pulled - normed * row_dot[None, :] / full_width)...  7.06 us
  transfers between devices with their start and end apart: 3, of which 2 were waited for; matrix products, arithmetic and copies ran while one was open for 4% of the time, Pallas kernels for 0%

profile of v1, /device:TPU:0, one launch (start us, length us, event | category | flops | bytes accessed | tf_op | source)
XLA Modules:
  0.0 184.2 jit_solution(11629335155028974784)
XLA Ops:
  7.2 0.0 all-gather.4.cloned.1.call-start
  7.2 1.1 slice.26
  8.3 1.3 collective-permute-start.1
  9.6 0.8 copy.38
  10.4 0.1 reshape.66
  10.5 1.6 collective-permute-done.1.ga_ref
  12.1 13.9 %states.1 = (f32[128,16,128]{2,1,0:T(8,128)S(1)}, f32[128,16,128]{2,1,0:T(8,128)S(1)}, f32[16,32,128]{2,1,0:T(8,128)}) custom-call(f32[16,1,128]{2,1,0:T(1,128)S(1)} %bitcast.18, bf16[2048,1024]{1,0:T(8,128)(2,1)} %g_ref.3, bf16[2048,128]{1,0:T(8,128)(2,1)S(1)} %collective-permute-done.1.ga_ref), custom_call_target="tpu_custom_call" | custom-call | flops 268435456 | bytes 8388608 | tf_op jit(solution)/shard_map/states/pallas_call | solution.py:246
  26.1 0.0 all-gather.4.cloned.1.call-update
  26.1 1.9 %slice.24 = bf16[2048,128]{1,0:T(8,128)(2,1)} slice(bf16[2048,1024]{1,0:T(8,128)(2,1)} %h_ref.1), slice={[0:2048], [896:1024]} | slice | bytes 1048576 | tf_op jit(solution)/shard_map/slice | solution.py:221
  28.0 9.9 %collective-permute-start = (bf16[2048,128]{1,0:T(8,128)(2,1)}, bf16[2048,128]{1,0:T(8,128)(2,1)S(1)}, u32[]{:S(2)}, u32[]{:S(2)}) collective-permute-start(bf16[2048,128]{1,0:T(8,128)(2,1)} %slice.24), channel_id=1, source_target_pairs={{0,4},{4,8},{8,12},{12,16},{16,20},{20,24},{24,28},{1,5},{5,9},{9,... | collective-permute-start | bytes 1572872 | tf_op jit(solution)/shard_map/ppermute | solution.py:20
  37.9 0.8 convert_element_type.15.tap_ref
  38.7 0.8 copy.39
  39.5 0.1 reshape.67
  39.6 3.2 %fusion = f32[1024]{0:T(1024)S(1)} fusion(bf16[2048,1024]{1,0:T(8,128)(2,1)} %h_ref.1), kind=kLoop, calls=%fused_computation.2 | loop fusion | flops 6290432 | bytes 4198400 | tf_op jit(solution)/shard_map/reduce_sum | solution.py:226
  42.7 0.0 collective-permute-done.hb_ref
  42.7 0.3 multiply_reduce_fusion
  43.0 12.1 %psum.14 = f32[1152]{0:T(1024)S(1)} all-reduce(f32[1152]{0:T(1024)S(1)} %pad_maximum_fusion), channel_id=1, replica_groups=mesh['ctx'=8,'ch'=4] {'ch'}, use_global_device_ids=true, to_apply=%region_2.0 | all-reduce | flops 1152 | bytes 9216 | tf_op jit(solution)/shard_map/psum | solution.py:228
  55.1 9.1 %all-gather.4.cloned.1.call-done = f32[128,32,128]{2,1,0:T(8,128)} async-done(((f32[16,32,128]{2,1,0:T(8,128)}), f32[128,32,128]{2,1,0:T(8,128)}) %all-gather.4.cloned.1.call-update) | async-done | bytes 2097168 | tf_op jit(solution)/shard_map/all_gather | solution.py:258
  64.3 1.6 copy-done.1
  65.9 79.5 %main.1 = (f32[2048,1024]{1,0:T(8,128)}, f32[128,128]{1,0:T(8,128)S(1)}, f32[16,1,128]{2,1,0:T(1,128)S(1)}, f32[16,1,128]{2,1,0:T(1,128)S(1)}, f32[16,1,128]{2,1...) custom-call(s32[1]{0:T(128)} %bitcast.rank_ref, f32[16,1,128]{2,1,0:T(1,128)S(1)} %bitcast.19, ...), custom_call_target="tpu_custom_call" | custom-call | flops 6442450944 | bytes 25165824 | tf_op jit(solution)/shard_map/main/pallas_call | solution.py:261
  145.4 10.4 %all-gather.1 = f32[1536,128]{1,0:T(8,128)S(1)} all-gather(f32[192,128]{1,0:T(8,128)S(1)} %constant_dynamic-update-slice_fusion), channel_id=3, replica_groups=mesh['ctx'=8,'ch'=4] {'ctx'}, dimensions={0}, use_global_device_ids=true | all-gather | bytes 884736 | tf_op jit(solution)/shard_map/all_gather | solution.py:301
  155.8 0.6 fusion.6
  156.4 0.6 slice_multiply_fusion
  157.1 11.7 %psum.15 = f32[1024]{0:T(1024)S(1)} all-reduce(f32[1024]{0:T(1024)S(1)} %bitcast.29), channel_id=1, replica_groups=mesh['ctx'=8,'ch'=4] {'ch'}, use_global_device_ids=true, to_apply=%region_4.0 | all-reduce | flops 1024 | bytes 8192 | tf_op jit(solution)/shard_map/psum | solution.py:295
  168.8 0.6 divide_multiply_fusion
  169.4 0.1 reshape.78
  169.4 0.1 copy.45
  169.5 0.1 reshape.77
  169.6 0.1 copy.43
  169.7 7.1 %fusion.5 = bf16[2048,1024]{1,0:T(8,128)(2,1)} fusion(bf16[2048,1024]{1,0:T(8,128)(2,1)} %h_ref.1, f32[2048,1024]{1,0:T(8,128)} %get-tuple-element.20, f32[1024]{0:T(1024)S(1)} %psum.15, f32[2048]{0:T(1024)S(1)} %copy-done, f32[1024]{0:T(1024)S(1)} %get-tuple-element.48), kind=kLoop, calls=%fused_computation.7 | loop fusion | flops 16777216 | bytes 16793600 | tf_op jit(solution)/shard_map/convert_element_type | solution.py:312
  176.7 0.0 copy-done.4
  176.7 0.6 multiply_multiply_fusion
  (18 shorter events, 0.1 us)
Async XLA Ops:
  7.2 57.1 %copy-start = (f32[2048]{0:T(1024)S(1)}, f32[2048]{0:T(1024)}, u32[]{:S(2)}) copy-start(f32[2048]{0:T(1024)} %param.9) | copy-start | bytes 24580
  7.2 57.1 %copy-start.2 = (f32[2048]{0:T(1024)S(1)}, f32[2048]{0:T(1024)}, u32[]{:S(2)}) copy-start(f32[2048]{0:T(1024)} %param.13) | copy-start | bytes 24580
  7.2 57.1 %all-gather.4.cloned.1.call-start = ((), (), s32[]{:S(2)}) async-start(), calls=%async_computation | async-start | bytes 2359296 | tf_op jit(solution)/shard_map/all_gather | solution.py:258
  8.3 3.8 %collective-permute-start.1 = (bf16[2048,128]{1,0:T(8,128)(2,1)S(1)}, bf16[2048,128]{1,0:T(8,128)(2,1)S(1)}, u32[]{:S(2)}, u32[]{:S(2)}) collective-permute-start(bf16[2048,128]{1,0:T(8,128)(2,1)S(1)} %slice.26), channel_id=1, source_target_pairs={{4,0},{8,4},{12,8},{16,12},{20,16},{24,20},{28,24},{5,1},{9,5},{13... | collective-permute-start | bytes 1572872 | tf_op jit(solution)/shard_map/ppermute | solution.py:20
  28.0 14.8 %collective-permute-start = (bf16[2048,128]{1,0:T(8,128)(2,1)}, bf16[2048,128]{1,0:T(8,128)(2,1)S(1)}, u32[]{:S(2)}, u32[]{:S(2)}) collective-permute-start(bf16[2048,128]{1,0:T(8,128)(2,1)} %slice.24), channel_id=1, source_target_pairs={{0,4},{4,8},{8,12},{12,16},{16,20},{20,24},{24,28},{1,5},{5,9},{9,... | collective-permute-start | bytes 1572872 | tf_op jit(solution)/shard_map/ppermute | solution.py:20
  64.3 1.6 copy-start.1
  169.7 7.1 %copy-start.3 = (f32[128,16]{0,1:T(8,128)S(1)}, f32[128,16]{0,1:T(8,128)}, u32[]{:S(2)}) copy-start(f32[128,16]{0,1:T(8,128)} %param.12) | copy-start | bytes 24580
  169.7 7.1 %copy-start.4 = (f32[128,16]{0,1:T(8,128)S(1)}, f32[128,16]{0,1:T(8,128)}, u32[]{:S(2)}) copy-start(f32[128,16]{0,1:T(8,128)} %param.11) | copy-start | bytes 24580
Sparse Core Ops, SparseCore 0:
  26.2 38.0 all-gather.3

commit v2 on v1

--- a/solution.py
+++ b/solution.py
@@ -18,6 +18,45 @@
     count = lax.axis_size(axis)
     pairs = [(i, i + by) for i in range(count) if 0 <= i + by < count]
     return lax.ppermute(x, axis, pairs)
+
+
+def exchanged(x, axis, bit):
+    count = lax.axis_size(axis)
+    return lax.ppermute(x, axis, [(i, i ^ bit) for i in range(count)])
+
+
+def sum_over(x, axis):
+    bit = 1
+    while bit < lax.axis_size(axis):
+        x = x + exchanged(x, axis, bit)
+        bit *= 2
+    return x
+
+
+def states_after(total, rates, tokens):
+    count = lax.axis_size("ctx")
+    rank = lax.axis_index("ctx")
+    into0 = jnp.zeros_like(rates)
+    into1 = jnp.zeros_like(rates)
+    bit = 1
+    while bit < count:
+        other = exchanged(total, "ctx", bit)
+        o0, o1 = other[:, :GW], other[:, GW:]
+        t0, t1 = total[:, :GW], total[:, GW:]
+        lower = (rank & bit) == 0
+        start = (rank // bit + 1) * bit
+        gap = ((start - rank - 1) * tokens).astype(jnp.float32)
+        factor = jnp.where(lower, jnp.exp(-rates * gap), 0.0)
+        into0 = into0 + factor * o0
+        into1 = into1 + factor * (o1 + gap * o0)
+        if 2 * bit < count:
+            span = float(bit * tokens)
+            decay = jnp.exp(-rates * span)
+            e0, e1 = jnp.where(lower, t0, o0), jnp.where(lower, t1, o1)
+            l0, l1 = jnp.where(lower, o0, t0), jnp.where(lower, o1, t1)
+            total = jnp.concatenate([e0 + decay * l0, e1 + decay * (l1 + span * l0)], axis=1)
+        bit *= 2
+    return jnp.concatenate([into0, into1], axis=1)
 
 
 def dot(a, b, ca, cb):
@@ -57,12 +96,13 @@
     return [ref[rows, W * k : W * (k + 1)] for k in range(blocks)]
 
 
-def state_kernel(rate_ref, g_ref, ga_ref, s0_ref, s1_ref, total_ref):
+def state_kernel(rate_ref, g_ref, ga_ref, s0_ref, s1_ref, total_ref, seg_rate_ref):
     blocks = g_ref.shape[1] // W
     rates = columns_of(rate_ref[0])
     lane_int = lax.broadcasted_iota(jnp.int32, (GW, W), 1)
     lane = lane_int.astype(jnp.float32)
     seg = lane_int // GW
+    rate_seg = jnp.zeros((GW, W), jnp.float32)
     total0 = jnp.zeros((GW, W), jnp.float32)
     total1 = jnp.zeros((GW, W), jnp.float32)
     for q in range(PACK):
@@ -86,21 +126,21 @@
         s0_ref[q] = s0
         s1_ref[q] = s1
         here = seg == q
+        rate_seg = jnp.where(here, r, rate_seg)
         total0 = jnp.where(here, pltpu.roll(s0, GW * q, 1) if q else s0, total0)
         total1 = jnp.where(here, pltpu.roll(s1, GW * q, 1) if q else s1, total1)
     total_ref[0, :GW] = total0
     total_ref[0, GW:] = total1
+    seg_rate_ref[0] = rate_seg
 
 
 def main_kernel(
-    rank_ref, rate_ref, res_ref, gain_ref, skip_ref, tap_ref, inv_ref, h_ref, hb_ref, g_ref, ga_ref,
-    s0_ref, s1_ref, total_ref,
+    rate_ref, res_ref, gain_ref, skip_ref, tap_ref, inv_ref, h_ref, hb_ref, g_ref, ga_ref,
+    s0_ref, s1_ref, into_ref,
     ig_ref, tapg_ref, mom0_ref, mom1_ref, skipg_ref, gaing_ref, dot_ref,
 ):
     tokens = g_ref.shape[1]
     blocks = tokens // W
-    count = total_ref.shape[0]
-    rank = rank_ref[0]
     rates = columns_of(rate_ref[0])
     residues = columns_of(res_ref[0])
     gains = columns_of(gain_ref[0])
@@ -111,18 +151,13 @@
     upper = lax.broadcasted_iota(jnp.int32, (W, W), 1) >= lax.broadcasted_iota(
         jnp.int32, (W, W), 0
     )
-    rate_seg = jnp.zeros((GW, W), jnp.float32)
-    for q in range(PACK):
-        rate_seg = jnp.where(seg == q, rates[GW * q : GW * (q + 1)], rate_seg)
-    in0 = jnp.zeros((GW, W), jnp.float32)
-    in1 = jnp.zeros((GW, W), jnp.float32)
-    for m in range(1, count):
-        gap = m - rank - 1
-        span = (jnp.maximum(gap, 0) * tokens).astype(jnp.float32)
-        factor = jnp.where(gap >= 0, jnp.exp(-rate_seg * span), 0.0)
-        t0 = total_ref[m, 0, :GW]
-        in0 = in0 + factor * t0
-        in1 = in1 + factor * (total_ref[m, 0, GW:] + span * t0)
+    lower = lax.broadcasted_iota(jnp.int32, (W, W), 1) <= lax.broadcasted_iota(
+        jnp.int32, (W, W), 0
+    )
+    back = jnp.where(lane_int == 0, 0.0, float(W) - lane)
+    gap = float(W) - lane
+    in0 = into_ref[0, :GW]
+    in1 = into_ref[0, GW:]
     left = ((blocks - seg) * W).astype(jnp.float32)
 
     @pl.when(pl.program_id(0) == 0)
@@ -139,9 +174,12 @@
         amp = residues[rows] * jnp.sqrt(2.0 * r)
         gain = gains[rows]
         skip = skips[rows]
-        fall = jnp.exp(-r * lane)
+        to_end = jnp.exp(-r * gap)
+        fall = jnp.where(lane_int == 0, 1.0, to_end)
         kern = jnp.sum(amp * fall, axis=0, keepdims=True)
-        kern_high, kern_low = split_two(jnp.where(upper, circulant(kern), 0.0))
+        kern_two = jnp.concatenate(
+            split_two(jnp.where(lower, circulant(kern), 0.0)), axis=0
+        )
         circ = circulant(tap_ref[q : q + 1, :])
         now = jnp.where(upper, circ, 0.0).astype(jnp.bfloat16)
         before = jnp.where(upper, 0.0, circ).astype(jnp.bfloat16)
@@ -150,7 +188,8 @@
         unit_back = (hb_ref[rows, :].astype(jnp.float32) * inv_back * gain).astype(jnp.bfloat16)
         x_now = jnp.concatenate(units, axis=0)
         x_before = jnp.concatenate([unit_back] + units[:-1], axis=0)
-        mixed = (dot(x_now, now, 1, 0) + dot(x_before, before, 1, 0)).astype(jnp.bfloat16)
+        x_both = jnp.concatenate([x_now, x_before], axis=1)
+        mixed = dot(x_both, jnp.concatenate([now, before], axis=0), 1, 0).astype(jnp.bfloat16)
         g_tiles = tiles_of(g_ref, rows, blocks)
         grads = jnp.concatenate(g_tiles, axis=0)
         grads_long = jnp.concatenate(g_tiles + [ga_ref[rows, :]], axis=0)
@@ -162,8 +201,6 @@
         decay = jnp.exp(-r * left)
         after0 = s0_ref[q] + decay * a0in
         after1 = s1_ref[q] + decay * (a1in + left * a0in)
-        gap = float(W) - lane
-        to_end = jnp.exp(-r * gap)
         a_high, a_low = split_two(jnp.concatenate([after0, a0in], axis=1))
         w_high, w_low = split_two(amp * to_end)
         outer = dot(
@@ -173,23 +210,26 @@
         )[: W + GW]
         wide = grads_long.astype(jnp.float32)
         gm = (
-            dot(grads_long, kern_high, 1, 1)
-            + dot(grads_long, kern_low, 1, 1)
+            dot(jnp.concatenate([grads_long, grads_long], axis=1), kern_two, 1, 0)
             + outer
             + jnp.concatenate([skip] * (blocks + 1), axis=0) * wide
         ).astype(jnp.bfloat16)
         gm_now = gm[:W]
-        ig = dot(gm_now, now, 1, 1) + dot(gm[GW:], before, 1, 1)
-        pairs = jnp.where(upper, dot(x_now, gm_now, 0, 0), dot(x_before, gm_now, 0, 0))
-        tapg_ref[q : q + 1, :] = diagonal_sums(pairs)
-        lags = diagonal_sums(jnp.where(upper, dot(mixed, grads, 0, 0), 0.0))
+        ig = dot(
+            jnp.concatenate([gm_now, gm[GW:]], axis=1),
+            jnp.concatenate([now, before], axis=1),
+            1, 1,
+        )
+        pairs = dot(gm_now, x_both, 0, 0)
+        tapg_ref[q : q + 1, :] = diagonal_sums(jnp.where(lower, pairs[:, :W], pairs[:, W:]))
+        lags = diagonal_sums(jnp.where(lower, dot(grads, mixed, 0, 0), 0.0))
         table = jnp.concatenate(split_two(to_end) + split_two(to_end * gap), axis=0)
         lifted = dot(table, mixed, 1, 1)
         l0 = lifted[:GW] + lifted[GW : 2 * GW]
         l1 = lifted[2 * GW : 3 * GW] + lifted[3 * GW :]
         near = lags * fall
         moments0.append(l0 * after0 + near)
-        moments1.append(l1 * after0 + l0 * after1 + near * lane)
+        moments1.append(l1 * after0 + l0 * after1 + near * back)
         skip_terms = wide[:W] * mixed.astype(jnp.float32)
         gain_terms = ig * jnp.concatenate(normed, axis=0)
         skip_sum = skip_terms[:GW]
@@ -225,9 +265,7 @@
         wide = x.astype(f32)
         return jnp.sum(wide * wide, axis=0)
 
-    squares = lax.psum(
-        jnp.concatenate([squares_of(hidden_back), squares_of(hidden)]), "ch"
-    )
+    squares = sum_over(jnp.concatenate([squares_of(hidden_back), squares_of(hidden)]), "ch")
     inverse_all = lax.rsqrt(squares / full_width + eps_norm)
     inverse_rms = inverse_all[W:]
 
@@ -243,32 +281,38 @@
     row_shape = jax.ShapeDtypeStruct((steps, 1, W), f32)
     state_shape = jax.ShapeDtypeStruct((groups, GW, W), f32)
 
-    state0, state1, total = pl.pallas_call(
+    state0, state1, total, seg_rates = pl.pallas_call(
         state_kernel,
         grid=(steps,),
         in_specs=[row_spec, wide_spec, edge_spec],
-        out_specs=[state_spec, state_spec, pl.BlockSpec((1, 2 * GW, W), lambda i: (i, 0, 0))],
-        out_shape=[state_shape, state_shape, jax.ShapeDtypeStruct((steps, 2 * GW, W), f32)],
+        out_specs=[
+            state_spec, state_spec,
+            pl.BlockSpec((1, 2 * GW, W), lambda i: (i, 0, 0)),
+            pl.BlockSpec((1, GW, W), lambda i: (i, 0, 0)),
+        ],
+        out_shape=[
+            state_shape, state_shape,
+            jax.ShapeDtypeStruct((steps, 2 * GW, W), f32),
+            jax.ShapeDtypeStruct((steps, GW, W), f32),
+        ],
         compiler_params=pltpu.CompilerParams(vmem_limit_bytes=VMEM_LIMIT),
         cost_estimate=pl.CostEstimate(
             flops=groups * 2 * 64 * W * W, bytes_accessed=8 * 2**20, transcendentals=0
         ),
         name="states",
     )(rate_rows, cotangent, cot_ahead)
-    totals = lax.all_gather(total, "ctx", axis=0, tiled=False)
-
-    rank = lax.axis_index("ctx").astype(jnp.int32).reshape(1)
+    into = states_after(total, seg_rates, tokens)
+
     input_grad, tap_part, mom0, mom1, skip_part, gain_part, dots = pl.pallas_call(
         main_kernel,
         grid=(steps,),
         in_specs=[
-            pl.BlockSpec(memory_space=pltpu.SMEM),
             row_spec, row_spec, row_spec, row_spec,
             pl.BlockSpec((PACK, W), lambda i: (i, 0)),
             pl.BlockSpec((1, tokens + W), lambda i: (0, 0)),
             wide_spec, edge_spec, wide_spec, edge_spec,
             state_spec, state_spec,
-            pl.BlockSpec((ctx_count, 1, 2 * GW, W), lambda i: (0, i, 0, 0)),
+            pl.BlockSpec((1, 2 * GW, W), lambda i: (i, 0, 0)),
         ],
         out_specs=[
             wide_spec,
@@ -288,18 +332,16 @@
         ),
         name="main",
     )(
-        rank, rate_rows, residue_rows, gain_rows, skip_rows, mr_filter.astype(f32),
+        rate_rows, residue_rows, gain_rows, skip_rows, mr_filter.astype(f32),
         inverse_all.reshape(1, tokens + W), hidden, hidden_back, cotangent, cot_ahead,
-        state0, state1, totals,
-    )
-    row_dot = lax.psum(
-        jnp.sum(dots.reshape(tokens // W, GW, W), axis=1).reshape(tokens), "ch"
-    )
+        state0, state1, into,
+    )
+    row_dot = sum_over(jnp.sum(dots.reshape(tokens // W, GW, W), axis=1).reshape(tokens), "ch")
     parts = jnp.concatenate(
         [tap_part] + [x.reshape(steps, W) for x in (mom0, mom1, skip_part, gain_part)], axis=0
     )
-    whole = jnp.sum(lax.all_gather(parts, "ctx", axis=0, tiled=False), axis=0)
-    tap_total = whole[:groups]
+    whole = sum_over(parts, "ctx")
+    tap_total = jnp.roll(whole[:groups, ::-1], 1, axis=1)
     first, second, skip_total, gain_total = (
         whole[groups + steps * i : groups + steps * (i + 1)] for i in range(4)
     )

time: 185 us -> 159 us (0.86)
  blocking collectives: 34.2 us -> 0 us
  starting transfers between devices: 11.3 us -> 27.5 us
  between operations: 14.2 us -> 0.86 us
  other arithmetic: 13.8 us -> 17.7 us
    ppermute x0 -> x10, starting transfers between devices: none -> 24.2 us  [exchanged(): return lax.ppermute(x, axis, [(i, i ^ bit) for i in range(count)])]
    psum x2 -> x0, blocking collectives: 23.8 us -> none  [the longest x1 12.1 us: local(): lax.psum(jnp.concatenate([squares_of(hidden_back), squares_of(hidden)]),...]
    ppermute x0 -> x10, waiting for transfers between devices: none -> 10.8 us  [exchanged(): return lax.ppermute(x, axis, [(i, i ^ bit) for i in range(count)])]
    all_gather x1 -> x0, blocking collectives: 10.4 us -> none  [local(): whole = jnp.sum(lax.all_gather(parts, 'ctx', axis=0, tiled=False), axis=0)]
    all_gather x1 -> x0, waiting for transfers between devices: 9.12 us -> none  [local(): totals = lax.all_gather(total, 'ctx', axis=0, tiled=False)]
    ppermute x2, starting transfers between devices: 11.2 us -> 3.24 us  [passed_along(): return lax.ppermute(x, axis, pairs)]
    add x0 -> x8, other arithmetic: none -> 3.59 us  [the longest x2 2.2 us: states_after(): e0 + decay * l0]
  transfers between devices with their start and end apart: 3 -> 12, of which waited for: 2 -> 6; matrix products, arithmetic and copies ran while one was open for 4% -> 11% of each run, Pallas kernels for 0% -> 0%
where the time goes in v2:
time: 159 us
  Pallas kernels  94.5 us (59%)
  starting transfers between devices  27.5 us (17%)
  other arithmetic  17.7 us (11%)
  waiting for transfers between devices  12.4 us (8%)
  local copies, waits for them, and re-layouts  5.84 us (4%)
    pallas_call x1, Pallas kernels, local(): pl.pallas_call(main_kernel, grid=(steps,), in_specs=[row_spec, row_spec,...  81.2 us
    ppermute x10, starting transfers between devices, exchanged(): return lax.ppermute(x, axis, [(i, i ^ bit) for i in range(count)])  24.2 us
    pallas_call x1, Pallas kernels, local(): pl.pallas_call(state_kernel, grid=(steps,), in_specs=[row_spec, wide_spec...  13.3 us
    ppermute x10, waiting for transfers between devices, exchanged(): return lax.ppermute(x, axis, [(i, i ^ bit) for i in range(count)])  10.8 us
    convert_element_type x1, other arithmetic, local(): (inverse_rms[None, :] * (pulled - normed * row_dot[None, :] / full_width)...  5.88 us
    reduce_sum x2, other arithmetic, squares_of(): return jnp.sum(wide * wide, axis=0)  3.4 us
    ppermute x2, starting transfers between devices, passed_along(): return lax.ppermute(x, axis, pairs)  3.24 us
  transfers between devices with their start and end apart: 12, of which 6 were waited for; matrix products, arithmetic and copies ran while one was open for 11% of the time, Pallas kernels for 0%

profile of v2, /device:TPU:0, one launch (start us, length us, event | category | flops | bytes accessed | tf_op | source)
XLA Modules:
  0.0 158.7 jit_solution(17848949839078631570)
XLA Ops:
  0.6 1.1 slice.62
  1.7 1.3 collective-permute-start.3
  3.0 0.8 copy.30
  3.9 1.6 %collective-permute-done.3.ga_ref = bf16[2048,128]{1,0:T(8,128)(2,1)S(1)} collective-permute-done((bf16[2048,128]{1,0:T(8,128)(2,1)S(1)}, bf16[2048,128]{1,0:T(8,128)(2,1)S(1)}, u32[]{:S(2)}, u32[]{:S(2)}) %collective-permute-start.3) | collective-permute-done | bytes 524320 | tf_op jit(solution)/shard_map/ppermute | solution.py:20
  5.5 13.3 %states.1 = (f32[128,16,128]{2,1,0:T(8,128)S(1)}, f32[128,16,128]{2,1,0:T(8,128)S(1)}, f32[16,32,128]{2,1,0:T(8,128)S(1)}, f32[16,16,128]{2,1,0:T(8,128)S(1)}) custom-call(f32[16,1,128]{2,1,0:T(1,128)S(1)} %bitcast.16, bf16[2048,1024]{1,0:T(8,128)(2,1)} %g_ref.3, bf16[2048,128]{1,0:T(8,128)(2,1)S(1)} %collective-permute-done.3.ga_ref), custom_call_target="tpu_custom_call" | custom-call | flops 268435456 | bytes 8388608 | tf_op jit(solution)/shard_map/states/pallas_call | solution.py:284
  18.8 8.1 %collective-permute-start.4 = (f32[16,32,128]{2,1,0:T(8,128)S(1)}, f32[16,32,128]{2,1,0:T(8,128)}, u32[]{:S(2)}, u32[]{:S(2)}) collective-permute-start(f32[16,32,128]{2,1,0:T(8,128)S(1)} %get-tuple-element.21), channel_id=1, source_target_pairs={{0,4},{4,0},{8,12},{12,8},{16,20},{20,16},{24,28},{28,24},{1,5},{5... | collective-permute-start | bytes 786440 | tf_op jit(solution)/shard_map/ppermute | solution.py:25
  26.9 1.9 %slice.60 = bf16[2048,128]{1,0:T(8,128)(2,1)} slice(bf16[2048,1024]{1,0:T(8,128)(2,1)} %h_ref.1), slice={[0:2048], [896:1024]} | slice | bytes 1048576 | tf_op jit(solution)/shard_map/slice | solution.py:261
  28.8 1.9 %collective-permute-start = (bf16[2048,128]{1,0:T(8,128)(2,1)}, bf16[2048,128]{1,0:T(8,128)(2,1)S(1)}, u32[]{:S(2)}, u32[]{:S(2)}) collective-permute-start(bf16[2048,128]{1,0:T(8,128)(2,1)} %slice.60), channel_id=1, source_target_pairs={{0,4},{4,8},{8,12},{12,16},{16,20},{20,24},{24,28},{1,5},{5,9},{9,... | collective-permute-start | bytes 1572872 | tf_op jit(solution)/shard_map/ppermute | solution.py:20
  30.8 1.0 multiply_add_fusion.4
  31.8 0.6 copy-done.3
  32.4 0.7 pad_maximum_fusion
  33.2 2.3 %collective-permute-start.5 = (f32[16,32,128]{2,1,0:T(8,128)}, f32[16,32,128]{2,1,0:T(8,128)}, u32[]{:S(2)}, u32[]{:S(2)}) collective-permute-start(f32[16,32,128]{2,1,0:T(8,128)} %pad_maximum_fusion), channel_id=1, source_target_pairs={{0,8},{4,12},{8,0},{12,4},{16,24},{20,28},{24,16},{28,20},{1,9},{5... | collective-permute-start | bytes 786440 | tf_op jit(solution)/shard_map/ppermute | solution.py:25
  35.5 3.1 %fusion = f32[1024]{0:T(1024)S(1)} fusion(bf16[2048,1024]{1,0:T(8,128)(2,1)} %h_ref.1), kind=kLoop, calls=%fused_computation.2 | loop fusion | flops 6290432 | bytes 4198400 | tf_op jit(solution)/shard_map/reduce_sum | solution.py:266
  38.9 1.6 %collective-permute-start.1 = (f32[1152]{0:T(1024)S(1)}, f32[1152]{0:T(1024)S(1)}, u32[]{:S(2)}, u32[]{:S(2)}) collective-permute-start(f32[1152]{0:T(1024)S(1)} %pad_maximum_fusion.3), channel_id=1, source_target_pairs={{0,1},{1,0},{2,3},{3,2},{4,5},{5,4},{6,7},{7,6},{8,9},{9,8},{10,11... | collective-permute-start | bytes 13832 | tf_op jit(solution)/shard_map/ppermute | solution.py:25
  40.6 2.5 %collective-permute-done.5 = f32[16,32,128]{2,1,0:T(8,128)} collective-permute-done((f32[16,32,128]{2,1,0:T(8,128)}, f32[16,32,128]{2,1,0:T(8,128)}, u32[]{:S(2)}, u32[]{:S(2)}) %collective-permute-start.5) | collective-permute-done | bytes 262176 | tf_op jit(solution)/shard_map/ppermute | solution.py:25
  43.0 1.2 multiply_add_fusion.2
  44.2 0.7 pad_maximum_fusion.1
  44.9 3.6 %collective-permute-start.6 = (f32[16,32,128]{2,1,0:T(8,128)}, f32[16,32,128]{2,1,0:T(8,128)}, u32[]{:S(2)}, u32[]{:S(2)}) collective-permute-start(f32[16,32,128]{2,1,0:T(8,128)} %pad_maximum_fusion.1), channel_id=1, source_target_pairs={{0,16},{4,20},{8,24},{12,28},{16,0},{20,4},{24,8},{28,12},{1,17},{... | collective-permute-start | bytes 786440 | tf_op jit(solution)/shard_map/ppermute | solution.py:25
  48.5 2.7 %collective-permute-start.2 = (f32[1152]{0:T(1024)S(1)}, f32[1152]{0:T(1024)S(1)}, u32[]{:S(2)}, u32[]{:S(2)}) collective-permute-start(f32[1152]{0:T(1024)S(1)} %fusion.10), channel_id=1, source_target_pairs={{0,2},{1,3},{2,0},{3,1},{4,6},{5,7},{6,4},{7,5},{8,10},{9,11},{10,... | collective-permute-start | bytes 13832 | tf_op jit(solution)/shard_map/ppermute | solution.py:25
  51.2 0.8 convert_element_type.22.tap_ref
  52.0 0.8 copy.31
  53.2 2.5 %collective-permute-done.6 = f32[16,32,128]{2,1,0:T(8,128)} collective-permute-done((f32[16,32,128]{2,1,0:T(8,128)}, f32[16,32,128]{2,1,0:T(8,128)}, u32[]{:S(2)}, u32[]{:S(2)}) %collective-permute-start.6) | collective-permute-done | bytes 262176 | tf_op jit(solution)/shard_map/ppermute | solution.py:25
  55.7 1.3 multiply_add_fusion
  57.1 81.2 %main.1 = (f32[2048,1024]{1,0:T(8,128)}, f32[128,128]{1,0:T(8,128)S(1)}, f32[16,1,128]{2,1,0:T(1,128)S(1)}, f32[16,1,128]{2,1,0:T(1,128)S(1)}, f32[16,1,128]{2,1...) custom-call(f32[16,1,128]{2,1,0:T(1,128)S(1)} %bitcast.17, f32[16,1,128]{2,1,0:T(1,128)S(1)} %bitcast.19, ...), custom_call_target="tpu_custom_call" | custom-call | flops 6442450944 | bytes 25165824 | tf_op jit(solution)/shard_map/main/pallas_call | solution.py:306
  138.8 3.2 %collective-permute-done.7 = f32[1024]{0:T(1024)S(1)} collective-permute-done((f32[1024]{0:T(1024)S(1)}, f32[1024]{0:T(1024)S(1)}, u32[]{:S(2)}, u32[]{:S(2)}) %collective-permute-start.7) | collective-permute-done | bytes 4128 | tf_op jit(solution)/shard_map/ppermute | solution.py:25
  142.0 2.6 %collective-permute-start.8 = (f32[1024]{0:T(1024)S(1)}, f32[1024]{0:T(1024)S(1)}, u32[]{:S(2)}, u32[]{:S(2)}) collective-permute-start(f32[1024]{0:T(1024)S(1)} %bitcast_add_fusion), channel_id=1, source_target_pairs={{0,2},{1,3},{2,0},{3,1},{4,6},{5,7},{6,4},{7,5},{8,10},{9,11},{10,... | collective-permute-start | bytes 12296 | tf_op jit(solution)/shard_map/ppermute | solution.py:25
  144.6 1.9 %collective-permute-start.10 = (f32[192,128]{1,0:T(8,128)S(1)}, f32[192,128]{1,0:T(8,128)S(1)}, u32[]{:S(2)}, u32[]{:S(2)}) collective-permute-start(f32[192,128]{1,0:T(8,128)S(1)} %add.100), channel_id=1, source_target_pairs={{0,8},{4,12},{8,0},{12,4},{16,24},{20,28},{24,16},{28,20},{1,9},{5... | collective-permute-start | bytes 294920 | tf_op jit(solution)/shard_map/ppermute | solution.py:25
  147.1 2.2 %collective-permute-done.10 = f32[192,128]{1,0:T(8,128)S(1)} collective-permute-done((f32[192,128]{1,0:T(8,128)S(1)}, f32[192,128]{1,0:T(8,128)S(1)}, u32[]{:S(2)}, u32[]{:S(2)}) %collective-permute-start.10) | collective-permute-done | bytes 98336 | tf_op jit(solution)/shard_map/ppermute | solution.py:25
  149.3 1.0 collective-permute-start.11
  150.4 5.9 %fusion.5 = bf16[2048,1024]{1,0:T(8,128)(2,1)} fusion(bf16[2048,1024]{1,0:T(8,128)(2,1)S(1)} %copy-done.2, f32[2048,1024]{1,0:T(8,128)} %get-tuple-element.22, f32[1024]{0:T(1024)S(1)} %get-tuple-element.37, f32[2048]{0:T(1024)S(1)} %copy-done, f32[1024]{0:T(1024)S(1)} %get-tuple-element.50), kind=kLoop, calls=%fused_computation.7 | loop fusion | flops 16777216 | bytes 16793600 | tf_op jit(solution)/shard_map/convert_element_type | solution.py:354
  157.4 0.6 multiply_multiply_fusion
  158.0 0.7 maximum_multiply_fusion
  (49 shorter events, 3.1 us)
Async XLA Ops:
  0.6 56.4 %copy-start = (f32[2048]{0:T(1024)S(1)}, f32[2048]{0:T(1024)}, u32[]{:S(2)}) copy-start(f32[2048]{0:T(1024)} %param.9) | copy-start | bytes 24580
  1.7 3.8 %collective-permute-start.3 = (bf16[2048,128]{1,0:T(8,128)(2,1)S(1)}, bf16[2048,128]{1,0:T(8,128)(2,1)S(1)}, u32[]{:S(2)}, u32[]{:S(2)}) collective-permute-start(bf16[2048,128]{1,0:T(8,128)(2,1)S(1)} %slice.62), channel_id=1, source_target_pairs={{4,0},{8,4},{12,8},{16,12},{20,16},{24,20},{28,24},{5,1},{9,5},{13... | collective-permute-start | bytes 1572872 | tf_op jit(solution)/shard_map/ppermute | solution.py:20
  18.8 11.9 %collective-permute-start.4 = (f32[16,32,128]{2,1,0:T(8,128)S(1)}, f32[16,32,128]{2,1,0:T(8,128)}, u32[]{:S(2)}, u32[]{:S(2)}) collective-permute-start(f32[16,32,128]{2,1,0:T(8,128)S(1)} %get-tuple-element.21), channel_id=1, source_target_pairs={{0,4},{4,0},{8,12},{12,8},{16,20},{20,16},{24,28},{28,24},{1,5},{5... | collective-permute-start | bytes 786440 | tf_op jit(solution)/shard_map/ppermute | solution.py:25
  28.8 9.8 %collective-permute-start = (bf16[2048,128]{1,0:T(8,128)(2,1)}, bf16[2048,128]{1,0:T(8,128)(2,1)S(1)}, u32[]{:S(2)}, u32[]{:S(2)}) collective-permute-start(bf16[2048,128]{1,0:T(8,128)(2,1)} %slice.60), channel_id=1, source_target_pairs={{0,4},{4,8},{8,12},{12,16},{16,20},{20,24},{24,28},{1,5},{5,9},{9,... | collective-permute-start | bytes 1572872 | tf_op jit(solution)/shard_map/ppermute | solution.py:20
  31.8 0.7 copy-start.3
  31.8 1.4 copy-start.4
  31.8 25.3 %copy-start.1 = (f32[2048]{0:T(1024)S(1)}, f32[2048]{0:T(1024)}, u32[]{:S(2)}) copy-start(f32[2048]{0:T(1024)} %param.13) | copy-start | bytes 24580
  33.2 9.9 %collective-permute-start.5 = (f32[16,32,128]{2,1,0:T(8,128)}, f32[16,32,128]{2,1,0:T(8,128)}, u32[]{:S(2)}, u32[]{:S(2)}) collective-permute-start(f32[16,32,128]{2,1,0:T(8,128)} %pad_maximum_fusion), channel_id=1, source_target_pairs={{0,8},{4,12},{8,0},{12,4},{16,24},{20,28},{24,16},{28,20},{1,9},{5... | collective-permute-start | bytes 786440 | tf_op jit(solution)/shard_map/ppermute | solution.py:25
  38.9 9.6 %collective-permute-start.1 = (f32[1152]{0:T(1024)S(1)}, f32[1152]{0:T(1024)S(1)}, u32[]{:S(2)}, u32[]{:S(2)}) collective-permute-start(f32[1152]{0:T(1024)S(1)} %pad_maximum_fusion.3), channel_id=1, source_target_pairs={{0,1},{1,0},{2,3},{3,2},{4,5},{5,4},{6,7},{7,6},{8,9},{9,8},{10,11... | collective-permute-start | bytes 13832 | tf_op jit(solution)/shard_map/ppermute | solution.py:25
  44.9 10.8 %collective-permute-start.6 = (f32[16,32,128]{2,1,0:T(8,128)}, f32[16,32,128]{2,1,0:T(8,128)}, u32[]{:S(2)}, u32[]{:S(2)}) collective-permute-start(f32[16,32,128]{2,1,0:T(8,128)} %pad_maximum_fusion.1), channel_id=1, source_target_pairs={{0,16},{4,20},{8,24},{12,28},{16,0},{20,4},{24,8},{28,12},{1,17},{... | collective-permute-start | bytes 786440 | tf_op jit(solution)/shard_map/ppermute | solution.py:25
  48.5 4.6 %collective-permute-start.2 = (f32[1152]{0:T(1024)S(1)}, f32[1152]{0:T(1024)S(1)}, u32[]{:S(2)}, u32[]{:S(2)}) collective-permute-start(f32[1152]{0:T(1024)S(1)} %fusion.10), channel_id=1, source_target_pairs={{0,2},{1,3},{2,0},{3,1},{4,6},{5,7},{6,4},{7,5},{8,10},{9,11},{10,... | collective-permute-start | bytes 13832 | tf_op jit(solution)/shard_map/ppermute | solution.py:25
  57.1 93.3 %copy-start.2 = (bf16[2048,1024]{1,0:T(8,128)(2,1)S(1)}, bf16[2048,1024]{1,0:T(8,128)(2,1)}, u32[]{:S(2)}) copy-start(bf16[2048,1024]{1,0:T(8,128)(2,1)} %h_ref.1) | copy-start | bytes 12582916
  138.3 3.7 %collective-permute-start.7 = (f32[1024]{0:T(1024)S(1)}, f32[1024]{0:T(1024)S(1)}, u32[]{:S(2)}, u32[]{:S(2)}) collective-permute-start(f32[1024]{0:T(1024)S(1)} %bitcast.25), channel_id=1, source_target_pairs={{0,1},{1,0},{2,3},{3,2},{4,5},{5,4},{6,7},{7,6},{8,9},{9,8},{10,11... | collective-permute-start | bytes 12296 | tf_op jit(solution)/shard_map/ppermute | solution.py:25
  138.5 6.1 %collective-permute-start.9 = (f32[192,128]{1,0:T(8,128)S(1)}, f32[192,128]{1,0:T(8,128)S(1)}, u32[]{:S(2)}, u32[]{:S(2)}) collective-permute-start(f32[192,128]{1,0:T(8,128)S(1)} %constant_dynamic-update-slice_fusion), channel_id=1, source_target_pairs={{0,4},{4,0},{8,12},{12,8},{16,20},{20,16},{24,28},{28,24},{1,5},{5... | collective-permute-start | bytes 294920 | tf_op jit(solution)/shard_map/ppermute | solution.py:25
  142.0 4.5 %collective-permute-start.8 = (f32[1024]{0:T(1024)S(1)}, f32[1024]{0:T(1024)S(1)}, u32[]{:S(2)}, u32[]{:S(2)}) collective-permute-start(f32[1024]{0:T(1024)S(1)} %bitcast_add_fusion), channel_id=1, source_target_pairs={{0,2},{1,3},{2,0},{3,1},{4,6},{5,7},{6,4},{7,5},{8,10},{9,11},{10,... | collective-permute-start | bytes 12296 | tf_op jit(solution)/shard_map/ppermute | solution.py:25
  144.6 4.7 %collective-permute-start.10 = (f32[192,128]{1,0:T(8,128)S(1)}, f32[192,128]{1,0:T(8,128)S(1)}, u32[]{:S(2)}, u32[]{:S(2)}) collective-permute-start(f32[192,128]{1,0:T(8,128)S(1)} %add.100), channel_id=1, source_target_pairs={{0,8},{4,12},{8,0},{12,4},{16,24},{20,28},{24,16},{28,20},{1,9},{5... | collective-permute-start | bytes 294920 | tf_op jit(solution)/shard_map/ppermute | solution.py:25
  149.3 6.9 %collective-permute-start.11 = (f32[192,128]{1,0:T(8,128)S(1)}, f32[192,128]{1,0:T(8,128)S(1)}, u32[]{:S(2)}, u32[]{:S(2)}) collective-permute-start(f32[192,128]{1,0:T(8,128)S(1)} %add.101), channel_id=1, source_target_pairs={{0,16},{4,20},{8,24},{12,28},{16,0},{20,4},{24,8},{28,12},{1,17},{... | collective-permute-start | bytes 294920 | tf_op jit(solution)/shard_map/ppermute | solution.py:25
  150.4 7.0 %copy-start.5 = (f32[128,16]{0,1:T(8,128)S(1)}, f32[128,16]{0,1:T(8,128)}, u32[]{:S(2)}) copy-start(f32[128,16]{0,1:T(8,128)} %param.12) | copy-start | bytes 24580
  150.4 7.0 %copy-start.6 = (f32[128,16]{0,1:T(8,128)S(1)}, f32[128,16]{0,1:T(8,128)}, u32[]{:S(2)}) copy-start(f32[128,16]{0,1:T(8,128)} %param.11) | copy-start | bytes 24580

commit v3 on v2

--- a/solution.py
+++ b/solution.py
@@ -168,7 +168,7 @@
     inv = [inv_ref[:, W * (k + 1) : W * (k + 2)] for k in range(blocks)]
     moments0, moments1, skip_rows, gain_rows = [], [], [], []
     dots = None
-    for q in range(PACK):
+    def one_group(q):
         rows = slice(GW * q, GW * (q + 1))
         r = rates[rows]
         amp = residues[rows] * jnp.sqrt(2.0 * r)
@@ -188,8 +188,10 @@
         unit_back = (hb_ref[rows, :].astype(jnp.float32) * inv_back * gain).astype(jnp.bfloat16)
         x_now = jnp.concatenate(units, axis=0)
         x_before = jnp.concatenate([unit_back] + units[:-1], axis=0)
+        yield
         x_both = jnp.concatenate([x_now, x_before], axis=1)
         mixed = dot(x_both, jnp.concatenate([now, before], axis=0), 1, 0).astype(jnp.bfloat16)
+        yield
         g_tiles = tiles_of(g_ref, rows, blocks)
         grads = jnp.concatenate(g_tiles, axis=0)
         grads_long = jnp.concatenate(g_tiles + [ga_ref[rows, :]], axis=0)
@@ -201,6 +203,7 @@
         decay = jnp.exp(-r * left)
         after0 = s0_ref[q] + decay * a0in
         after1 = s1_ref[q] + decay * (a1in + left * a0in)
+        yield
         a_high, a_low = split_two(jnp.concatenate([after0, a0in], axis=1))
         w_high, w_low = split_two(amp * to_end)
         outer = dot(
@@ -214,19 +217,23 @@
             + outer
             + jnp.concatenate([skip] * (blocks + 1), axis=0) * wide
         ).astype(jnp.bfloat16)
+        yield
         gm_now = gm[:W]
         ig = dot(
             jnp.concatenate([gm_now, gm[GW:]], axis=1),
             jnp.concatenate([now, before], axis=1),
             1, 1,
         )
+        yield
         pairs = dot(gm_now, x_both, 0, 0)
         tapg_ref[q : q + 1, :] = diagonal_sums(jnp.where(lower, pairs[:, :W], pairs[:, W:]))
         lags = diagonal_sums(jnp.where(lower, dot(grads, mixed, 0, 0), 0.0))
+        yield
         table = jnp.concatenate(split_two(to_end) + split_two(to_end * gap), axis=0)
         lifted = dot(table, mixed, 1, 1)
         l0 = lifted[:GW] + lifted[GW : 2 * GW]
         l1 = lifted[2 * GW : 3 * GW] + lifted[3 * GW :]
+        yield
         near = lags * fall
         moments0.append(l0 * after0 + near)
         moments1.append(l1 * after0 + l0 * after1 + near * back)
@@ -243,6 +250,10 @@
         skip_rows.append(skip_sum)
         gain_rows.append(gain_sum)
         dot_ref[...] += gain_terms * jnp.concatenate([gain] * blocks, axis=0)
+    for base in range(0, PACK, 4):
+        running = [one_group(q) for q in range(base, base + 4)]
+        while running:
+            running = [group for group in running if next(group, True) is None]
     mom0_ref[0] = row_sums(jnp.concatenate(moments0, axis=0))
     mom1_ref[0] = row_sums(jnp.concatenate(moments1, axis=0))
     skipg_ref[0] = row_sums(jnp.concatenate(skip_rows, axis=0))

time: 159 us -> 159 us (level)
  no operation moved by 1% of the time
where the time goes in v3:
time: 159 us; the launch traced here: 158 us
  Pallas kernels  94 us (59%)
  starting transfers between devices  27.5 us (17%)
  other arithmetic  17.7 us (11%)
  waiting for transfers between devices  12.4 us (8%)
  local copies, waits for them, and re-layouts  5.84 us (4%)
    pallas_call x1, Pallas kernels, local(): pl.pallas_call(main_kernel, grid=(steps,), in_specs=[row_spec, row_spec,...  80.7 us
    ppermute x10, starting transfers between devices, exchanged(): return lax.ppermute(x, axis, [(i, i ^ bit) for i in range(count)])  24.2 us
    pallas_call x1, Pallas kernels, local(): pl.pallas_call(state_kernel, grid=(steps,), in_specs=[row_spec, wide_spec...  13.3 us
    ppermute x10, waiting for transfers between devices, exchanged(): return lax.ppermute(x, axis, [(i, i ^ bit) for i in range(count)])  10.8 us
    convert_element_type x1, other arithmetic, local(): (inverse_rms[None, :] * (pulled - normed * row_dot[None, :] / full_width)...  5.88 us
    reduce_sum x2, other arithmetic, squares_of(): return jnp.sum(wide * wide, axis=0)  3.4 us
    ppermute x2, starting transfers between devices, passed_along(): return lax.ppermute(x, axis, pairs)  3.24 us
  transfers between devices with their start and end apart: 12, of which 6 were waited for; matrix products, arithmetic and copies ran while one was open for 11% of the time, Pallas kernels for 0%

profile of v3, /device:TPU:0, one launch (start us, length us, event | category | flops | bytes accessed | tf_op | source)
XLA Modules:
  0.0 158.2 jit_solution(13461670533437400357)
XLA Ops:
  0.6 1.1 slice.62
  1.7 1.3 collective-permute-start.3
  3.0 0.8 copy.30
  3.9 1.6 %collective-permute-done.3.ga_ref = bf16[2048,128]{1,0:T(8,128)(2,1)S(1)} collective-permute-done((bf16[2048,128]{1,0:T(8,128)(2,1)S(1)}, bf16[2048,128]{1,0:T(8,128)(2,1)S(1)}, u32[]{:S(2)}, u32[]{:S(2)}) %collective-permute-start.3) | collective-permute-done | bytes 524320 | tf_op jit(solution)/shard_map/ppermute | solution.py:20
  5.5 13.3 %states.1 = (f32[128,16,128]{2,1,0:T(8,128)S(1)}, f32[128,16,128]{2,1,0:T(8,128)S(1)}, f32[16,32,128]{2,1,0:T(8,128)S(1)}, f32[16,16,128]{2,1,0:T(8,128)S(1)}) custom-call(f32[16,1,128]{2,1,0:T(1,128)S(1)} %bitcast.16, bf16[2048,1024]{1,0:T(8,128)(2,1)} %g_ref.3, bf16[2048,128]{1,0:T(8,128)(2,1)S(1)} %collective-permute-done.3.ga_ref), custom_call_target="tpu_custom_call" | custom-call | flops 268435456 | bytes 8388608 | tf_op jit(solution)/shard_map/states/pallas_call | solution.py:295
  18.8 8.1 %collective-permute-start.4 = (f32[16,32,128]{2,1,0:T(8,128)S(1)}, f32[16,32,128]{2,1,0:T(8,128)}, u32[]{:S(2)}, u32[]{:S(2)}) collective-permute-start(f32[16,32,128]{2,1,0:T(8,128)S(1)} %get-tuple-element.21), channel_id=1, source_target_pairs={{0,4},{4,0},{8,12},{12,8},{16,20},{20,16},{24,28},{28,24},{1,5},{5... | collective-permute-start | bytes 786440 | tf_op jit(solution)/shard_map/ppermute | solution.py:25
  26.9 1.9 %slice.60 = bf16[2048,128]{1,0:T(8,128)(2,1)} slice(bf16[2048,1024]{1,0:T(8,128)(2,1)} %h_ref.1), slice={[0:2048], [896:1024]} | slice | bytes 1048576 | tf_op jit(solution)/shard_map/slice | solution.py:272
  28.8 1.9 %collective-permute-start = (bf16[2048,128]{1,0:T(8,128)(2,1)}, bf16[2048,128]{1,0:T(8,128)(2,1)S(1)}, u32[]{:S(2)}, u32[]{:S(2)}) collective-permute-start(bf16[2048,128]{1,0:T(8,128)(2,1)} %slice.60), channel_id=1, source_target_pairs={{0,4},{4,8},{8,12},{12,16},{16,20},{20,24},{24,28},{1,5},{5,9},{9,... | collective-permute-start | bytes 1572872 | tf_op jit(solution)/shard_map/ppermute | solution.py:20
  30.8 1.0 multiply_add_fusion.4
  31.8 0.6 copy-done.3
  32.4 0.7 pad_maximum_fusion
  33.2 2.3 %collective-permute-start.5 = (f32[16,32,128]{2,1,0:T(8,128)}, f32[16,32,128]{2,1,0:T(8,128)}, u32[]{:S(2)}, u32[]{:S(2)}) collective-permute-start(f32[16,32,128]{2,1,0:T(8,128)} %pad_maximum_fusion), channel_id=1, source_target_pairs={{0,8},{4,12},{8,0},{12,4},{16,24},{20,28},{24,16},{28,20},{1,9},{5... | collective-permute-start | bytes 786440 | tf_op jit(solution)/shard_map/ppermute | solution.py:25
  35.5 3.1 %fusion = f32[1024]{0:T(1024)S(1)} fusion(bf16[2048,1024]{1,0:T(8,128)(2,1)} %h_ref.1), kind=kLoop, calls=%fused_computation.2 | loop fusion | flops 6290432 | bytes 4198400 | tf_op jit(solution)/shard_map/reduce_sum | solution.py:277
  38.9 1.6 %collective-permute-start.1 = (f32[1152]{0:T(1024)S(1)}, f32[1152]{0:T(1024)S(1)}, u32[]{:S(2)}, u32[]{:S(2)}) collective-permute-start(f32[1152]{0:T(1024)S(1)} %pad_maximum_fusion.3), channel_id=1, source_target_pairs={{0,1},{1,0},{2,3},{3,2},{4,5},{5,4},{6,7},{7,6},{8,9},{9,8},{10,11... | collective-permute-start | bytes 13832 | tf_op jit(solution)/shard_map/ppermute | solution.py:25
  40.6 2.5 %collective-permute-done.5 = f32[16,32,128]{2,1,0:T(8,128)} collective-permute-done((f32[16,32,128]{2,1,0:T(8,128)}, f32[16,32,128]{2,1,0:T(8,128)}, u32[]{:S(2)}, u32[]{:S(2)}) %collective-permute-start.5) | collective-permute-done | bytes 262176 | tf_op jit(solution)/shard_map/ppermute | solution.py:25
  43.0 1.2 multiply_add_fusion.2
  44.2 0.7 pad_maximum_fusion.1
  44.9 3.6 %collective-permute-start.6 = (f32[16,32,128]{2,1,0:T(8,128)}, f32[16,32,128]{2,1,0:T(8,128)}, u32[]{:S(2)}, u32[]{:S(2)}) collective-permute-start(f32[16,32,128]{2,1,0:T(8,128)} %pad_maximum_fusion.1), channel_id=1, source_target_pairs={{0,16},{4,20},{8,24},{12,28},{16,0},{20,4},{24,8},{28,12},{1,17},{... | collective-permute-start | bytes 786440 | tf_op jit(solution)/shard_map/ppermute | solution.py:25
  48.5 2.7 %collective-permute-start.2 = (f32[1152]{0:T(1024)S(1)}, f32[1152]{0:T(1024)S(1)}, u32[]{:S(2)}, u32[]{:S(2)}) collective-permute-start(f32[1152]{0:T(1024)S(1)} %fusion.10), channel_id=1, source_target_pairs={{0,2},{1,3},{2,0},{3,1},{4,6},{5,7},{6,4},{7,5},{8,10},{9,11},{10,... | collective-permute-start | bytes 13832 | tf_op jit(solution)/shard_map/ppermute | solution.py:25
  51.2 0.8 convert_element_type.22.tap_ref
  52.0 0.8 copy.31
  53.2 2.5 %collective-permute-done.6 = f32[16,32,128]{2,1,0:T(8,128)} collective-permute-done((f32[16,32,128]{2,1,0:T(8,128)}, f32[16,32,128]{2,1,0:T(8,128)}, u32[]{:S(2)}, u32[]{:S(2)}) %collective-permute-start.6) | collective-permute-done | bytes 262176 | tf_op jit(solution)/shard_map/ppermute | solution.py:25
  55.7 1.3 multiply_add_fusion
  57.1 80.7 %main.1 = (f32[2048,1024]{1,0:T(8,128)}, f32[128,128]{1,0:T(8,128)S(1)}, f32[16,1,128]{2,1,0:T(1,128)S(1)}, f32[16,1,128]{2,1,0:T(1,128)S(1)}, f32[16,1,128]{2,1...) custom-call(f32[16,1,128]{2,1,0:T(1,128)S(1)} %bitcast.17, f32[16,1,128]{2,1,0:T(1,128)S(1)} %bitcast.19, ...), custom_call_target="tpu_custom_call" | custom-call | flops 6442450944 | bytes 25165824 | tf_op jit(solution)/shard_map/main/pallas_call | solution.py:317
  138.3 3.2 %collective-permute-done.7 = f32[1024]{0:T(1024)S(1)} collective-permute-done((f32[1024]{0:T(1024)S(1)}, f32[1024]{0:T(1024)S(1)}, u32[]{:S(2)}, u32[]{:S(2)}) %collective-permute-start.7) | collective-permute-done | bytes 4128 | tf_op jit(solution)/shard_map/ppermute | solution.py:25
  141.5 2.6 %collective-permute-start.8 = (f32[1024]{0:T(1024)S(1)}, f32[1024]{0:T(1024)S(1)}, u32[]{:S(2)}, u32[]{:S(2)}) collective-permute-start(f32[1024]{0:T(1024)S(1)} %bitcast_add_fusion), channel_id=1, source_target_pairs={{0,2},{1,3},{2,0},{3,1},{4,6},{5,7},{6,4},{7,5},{8,10},{9,11},{10,... | collective-permute-start | bytes 12296 | tf_op jit(solution)/shard_map/ppermute | solution.py:25
  144.1 1.9 %collective-permute-start.10 = (f32[192,128]{1,0:T(8,128)S(1)}, f32[192,128]{1,0:T(8,128)S(1)}, u32[]{:S(2)}, u32[]{:S(2)}) collective-permute-start(f32[192,128]{1,0:T(8,128)S(1)} %add.100), channel_id=1, source_target_pairs={{0,8},{4,12},{8,0},{12,4},{16,24},{20,28},{24,16},{28,20},{1,9},{5... | collective-permute-start | bytes 294920 | tf_op jit(solution)/shard_map/ppermute | solution.py:25
  146.6 2.2 %collective-permute-done.10 = f32[192,128]{1,0:T(8,128)S(1)} collective-permute-done((f32[192,128]{1,0:T(8,128)S(1)}, f32[192,128]{1,0:T(8,128)S(1)}, u32[]{:S(2)}, u32[]{:S(2)}) %collective-permute-start.10) | collective-permute-done | bytes 98336 | tf_op jit(solution)/shard_map/ppermute | solution.py:25
  148.8 1.0 collective-permute-start.11
  149.9 5.9 %fusion.5 = bf16[2048,1024]{1,0:T(8,128)(2,1)} fusion(bf16[2048,1024]{1,0:T(8,128)(2,1)S(1)} %copy-done.2, f32[2048,1024]{1,0:T(8,128)} %get-tuple-element.22, f32[1024]{0:T(1024)S(1)} %get-tuple-element.37, f32[2048]{0:T(1024)S(1)} %copy-done, f32[1024]{0:T(1024)S(1)} %get-tuple-element.50), kind=kLoop, calls=%fused_computation.7 | loop fusion | flops 16777216 | bytes 16793600 | tf_op jit(solution)/shard_map/convert_element_type | solution.py:365
  156.9 0.6 multiply_multiply_fusion
  157.5 0.7 maximum_multiply_fusion
  (49 shorter events, 3.1 us)
Async XLA Ops:
  0.6 56.4 %copy-start = (f32[2048]{0:T(1024)S(1)}, f32[2048]{0:T(1024)}, u32[]{:S(2)}) copy-start(f32[2048]{0:T(1024)} %param.9) | copy-start | bytes 24580
  1.7 3.8 %collective-permute-start.3 = (bf16[2048,128]{1,0:T(8,128)(2,1)S(1)}, bf16[2048,128]{1,0:T(8,128)(2,1)S(1)}, u32[]{:S(2)}, u32[]{:S(2)}) collective-permute-start(bf16[2048,128]{1,0:T(8,128)(2,1)S(1)} %slice.62), channel_id=1, source_target_pairs={{4,0},{8,4},{12,8},{16,12},{20,16},{24,20},{28,24},{5,1},{9,5},{13... | collective-permute-start | bytes 1572872 | tf_op jit(solution)/shard_map/ppermute | solution.py:20
  18.8 11.9 %collective-permute-start.4 = (f32[16,32,128]{2,1,0:T(8,128)S(1)}, f32[16,32,128]{2,1,0:T(8,128)}, u32[]{:S(2)}, u32[]{:S(2)}) collective-permute-start(f32[16,32,128]{2,1,0:T(8,128)S(1)} %get-tuple-element.21), channel_id=1, source_target_pairs={{0,4},{4,0},{8,12},{12,8},{16,20},{20,16},{24,28},{28,24},{1,5},{5... | collective-permute-start | bytes 786440 | tf_op jit(solution)/shard_map/ppermute | solution.py:25
  28.8 9.8 %collective-permute-start = (bf16[2048,128]{1,0:T(8,128)(2,1)}, bf16[2048,128]{1,0:T(8,128)(2,1)S(1)}, u32[]{:S(2)}, u32[]{:S(2)}) collective-permute-start(bf16[2048,128]{1,0:T(8,128)(2,1)} %slice.60), channel_id=1, source_target_pairs={{0,4},{4,8},{8,12},{12,16},{16,20},{20,24},{24,28},{1,5},{5,9},{9,... | collective-permute-start | bytes 1572872 | tf_op jit(solution)/shard_map/ppermute | solution.py:20
  31.8 0.7 copy-start.3
  31.8 1.4 copy-start.4
  31.8 25.3 %copy-start.1 = (f32[2048]{0:T(1024)S(1)}, f32[2048]{0:T(1024)}, u32[]{:S(2)}) copy-start(f32[2048]{0:T(1024)} %param.13) | copy-start | bytes 24580
  33.2 9.9 %collective-permute-start.5 = (f32[16,32,128]{2,1,0:T(8,128)}, f32[16,32,128]{2,1,0:T(8,128)}, u32[]{:S(2)}, u32[]{:S(2)}) collective-permute-start(f32[16,32,128]{2,1,0:T(8,128)} %pad_maximum_fusion), channel_id=1, source_target_pairs={{0,8},{4,12},{8,0},{12,4},{16,24},{20,28},{24,16},{28,20},{1,9},{5... | collective-permute-start | bytes 786440 | tf_op jit(solution)/shard_map/ppermute | solution.py:25
  38.9 9.6 %collective-permute-start.1 = (f32[1152]{0:T(1024)S(1)}, f32[1152]{0:T(1024)S(1)}, u32[]{:S(2)}, u32[]{:S(2)}) collective-permute-start(f32[1152]{0:T(1024)S(1)} %pad_maximum_fusion.3), channel_id=1, source_target_pairs={{0,1},{1,0},{2,3},{3,2},{4,5},{5,4},{6,7},{7,6},{8,9},{9,8},{10,11... | collective-permute-start | bytes 13832 | tf_op jit(solution)/shard_map/ppermute | solution.py:25
  44.9 10.8 %collective-permute-start.6 = (f32[16,32,128]{2,1,0:T(8,128)}, f32[16,32,128]{2,1,0:T(8,128)}, u32[]{:S(2)}, u32[]{:S(2)}) collective-permute-start(f32[16,32,128]{2,1,0:T(8,128)} %pad_maximum_fusion.1), channel_id=1, source_target_pairs={{0,16},{4,20},{8,24},{12,28},{16,0},{20,4},{24,8},{28,12},{1,17},{... | collective-permute-start | bytes 786440 | tf_op jit(solution)/shard_map/ppermute | solution.py:25
  48.5 4.6 %collective-permute-start.2 = (f32[1152]{0:T(1024)S(1)}, f32[1152]{0:T(1024)S(1)}, u32[]{:S(2)}, u32[]{:S(2)}) collective-permute-start(f32[1152]{0:T(1024)S(1)} %fusion.10), channel_id=1, source_target_pairs={{0,2},{1,3},{2,0},{3,1},{4,6},{5,7},{6,4},{7,5},{8,10},{9,11},{10,... | collective-permute-start | bytes 13832 | tf_op jit(solution)/shard_map/ppermute | solution.py:25
  57.1 92.8 %copy-start.2 = (bf16[2048,1024]{1,0:T(8,128)(2,1)S(1)}, bf16[2048,1024]{1,0:T(8,128)(2,1)}, u32[]{:S(2)}) copy-start(bf16[2048,1024]{1,0:T(8,128)(2,1)} %h_ref.1) | copy-start | bytes 12582916
  137.8 3.7 %collective-permute-start.7 = (f32[1024]{0:T(1024)S(1)}, f32[1024]{0:T(1024)S(1)}, u32[]{:S(2)}, u32[]{:S(2)}) collective-permute-start(f32[1024]{0:T(1024)S(1)} %bitcast.25), channel_id=1, source_target_pairs={{0,1},{1,0},{2,3},{3,2},{4,5},{5,4},{6,7},{7,6},{8,9},{9,8},{10,11... | collective-permute-start | bytes 12296 | tf_op jit(solution)/shard_map/ppermute | solution.py:25
  138.0 6.1 %collective-permute-start.9 = (f32[192,128]{1,0:T(8,128)S(1)}, f32[192,128]{1,0:T(8,128)S(1)}, u32[]{:S(2)}, u32[]{:S(2)}) collective-permute-start(f32[192,128]{1,0:T(8,128)S(1)} %constant_dynamic-update-slice_fusion), channel_id=1, source_target_pairs={{0,4},{4,0},{8,12},{12,8},{16,20},{20,16},{24,28},{28,24},{1,5},{5... | collective-permute-start | bytes 294920 | tf_op jit(solution)/shard_map/ppermute | solution.py:25
  141.5 4.5 %collective-permute-start.8 = (f32[1024]{0:T(1024)S(1)}, f32[1024]{0:T(1024)S(1)}, u32[]{:S(2)}, u32[]{:S(2)}) collective-permute-start(f32[1024]{0:T(1024)S(1)} %bitcast_add_fusion), channel_id=1, source_target_pairs={{0,2},{1,3},{2,0},{3,1},{4,6},{5,7},{6,4},{7,5},{8,10},{9,11},{10,... | collective-permute-start | bytes 12296 | tf_op jit(solution)/shard_map/ppermute | solution.py:25
  144.1 4.7 %collective-permute-start.10 = (f32[192,128]{1,0:T(8,128)S(1)}, f32[192,128]{1,0:T(8,128)S(1)}, u32[]{:S(2)}, u32[]{:S(2)}) collective-permute-start(f32[192,128]{1,0:T(8,128)S(1)} %add.100), channel_id=1, source_target_pairs={{0,8},{4,12},{8,0},{12,4},{16,24},{20,28},{24,16},{28,20},{1,9},{5... | collective-permute-start | bytes 294920 | tf_op jit(solution)/shard_map/ppermute | solution.py:25
  148.8 6.9 %collective-permute-start.11 = (f32[192,128]{1,0:T(8,128)S(1)}, f32[192,128]{1,0:T(8,128)S(1)}, u32[]{:S(2)}, u32[]{:S(2)}) collective-permute-start(f32[192,128]{1,0:T(8,128)S(1)} %add.101), channel_id=1, source_target_pairs={{0,16},{4,20},{8,24},{12,28},{16,0},{20,4},{24,8},{28,12},{1,17},{... | collective-permute-start | bytes 294920 | tf_op jit(solution)/shard_map/ppermute | solution.py:25
  149.8 7.0 %copy-start.5 = (f32[128,16]{0,1:T(8,128)S(1)}, f32[128,16]{0,1:T(8,128)}, u32[]{:S(2)}) copy-start(f32[128,16]{0,1:T(8,128)} %param.12) | copy-start | bytes 24580
  149.9 7.0 %copy-start.6 = (f32[128,16]{0,1:T(8,128)S(1)}, f32[128,16]{0,1:T(8,128)}, u32[]{:S(2)}) copy-start(f32[128,16]{0,1:T(8,128)} %param.11) | copy-start | bytes 24580
